TPU v7x, 32 devices: a whole 2x2x4 slice. The times are simulated.
32 devices in a mesh: dp: 8 (over z, x), mp: 4 (over y, core).
Axes of the slice: x: 2, y: 2, z: 4, core: 2. Of those that a mesh axis runs over, the one named last changes fastest.
Arguments:
- field_ids: int32 [26, 49152], P(None, 'dp'), may hold values from 0 to 4095
- field_present: int32 [26, 49152], P(None, 'dp'), may hold values 0 or 1
- dense_values: float32 [13, 49152], P(None, ('dp', 'mp')), may hold values from -6 to 6
- dense_present: int32 [13, 49152], P(None, ('dp', 'mp')), may hold values 0 or 1
- clicked: int32 [49152], P(('dp', 'mp')), may hold values 0 or 1
- tables: bfloat16 [4096, 1014], P('mp'), may hold values from -6 to 6
- cross_weight: bfloat16 [1027, 1027], replicated, may hold values from -0.1875 to 0.1875
- cross_bias: float32 [1027], replicated, may hold values from -3 to 3
- deep_weight: bfloat16 [1027, 1024], replicated, may hold values from -0.1875 to 0.1875
- deep_bias: float32 [1024], replicated, may hold values from -3 to 3
- head_cross: float32 [1027], replicated, may hold values from -0.125 to 0.125
- head_deep: float32 [1024], replicated, may hold values from -0.125 to 0.125
- head_bias: float32 [1], replicated, may hold values from -3 to 3
Outputs:
- logits: float32 [49152], P(('dp', 'mp'))
- loss: float32 [], replicated
- dense_grad: float32 [13, 49152], P(None, ('dp', 'mp'))
- tables_grad: float32 [4096, 1014], P(('mp', 'dp'))
- cross_weight_grad: float32 [1027, 1027], replicated
- cross_bias_grad: float32 [1027], replicated
- deep_weight_grad: float32 [1027, 1024], replicated
- deep_bias_grad: float32 [1024], replicated
- head_cross_grad: float32 [1027], replicated
- head_deep_grad: float32 [1024], replicated
- head_bias_grad: float32 [1], replicated
All inputs are finite; a program needn't handle non-finite values. No bound on the sum of `field_present` or of `dense_present` or of `clicked` on one device may be relied on, other than what follows from the above.
Results may differ from a plain program's by a relative error of at most 0.002.
Values may be sent and summed in bfloat16 or wider, within the bound.
No kernel may reach another device: no remote copies, remote signals or barrier semaphores. Data moves between devices by JAX's collectives and lax.ppermute only.
A program may use at most 128 MiB of HBM per device.

v0:
```python
from functools import partial
import math

import jax
import jax.numpy as jnp
from jax import lax
from jax.sharding import PartitionSpec as P


def lookup(local_ids, piece):
    fields = local_ids.shape[0]
    emb_width = piece.shape[1] // fields
    positions = lax.iota(jnp.int32, piece.shape[0])
    blocks = []
    for field in range(fields):
        onehot = (local_ids[field][:, None] == positions[None, :]).astype(jnp.bfloat16)
        blocks.append(
            jnp.dot(
                onehot,
                piece[:, field * emb_width : (field + 1) * emb_width],
                preferred_element_type=jnp.float32,
            )
        )
    return jnp.concatenate(blocks, axis=1)


def spread(local_ids, grads, out_rows):
    fields = local_ids.shape[0]
    emb_width = grads.shape[1] // fields
    positions = lax.iota(jnp.int32, out_rows)
    blocks = []
    for field in range(fields):
        onehot = (local_ids[field][:, None] == positions[None, :]).astype(jnp.bfloat16)
        blocks.append(
            lax.dot_general(
                onehot,
                grads[:, field * emb_width : (field + 1) * emb_width],
                (((0,), (0,)), ((), ())),
                preferred_element_type=jnp.float32,
            )
        )
    return jnp.concatenate(blocks, axis=1)


def contract_rows(left, right):
    return lax.dot_general(
        left, right, (((0,), (0,)), ((), ())), preferred_element_type=jnp.float32
    )


def contract_cols(left, right):
    return lax.dot_general(
        left, right, (((1,), (1,)), ((), ())), preferred_element_type=jnp.float32
    )


def body(
    field_ids,
    field_present,
    dense_values,
    dense_present,
    clicked,
    tables,
    cross_weight,
    cross_bias,
    deep_weight,
    deep_bias,
    head_cross,
    head_deep,
    head_bias,
):
    batch_group = field_ids.shape[1]
    table_rows = tables.shape[0]
    cat_width = tables.shape[1]
    chosen = jnp.where(field_present > 0, field_ids, 0)
    mp_index = lax.axis_index("mp")
    base_row = mp_index * table_rows
    part_ids = chosen - base_row
    embedded = lax.psum_scatter(
        lookup(part_ids, tables).astype(jnp.bfloat16), "mp", scatter_dimension=0, tiled=True
    ).astype(jnp.float32)
    present_mask = dense_present.astype(jnp.float32)
    x_zero = jnp.concatenate([embedded, (dense_values * present_mask).T], axis=1)
    x_low = x_zero.astype(jnp.bfloat16)
    cross_pre = jnp.dot(x_low, cross_weight, preferred_element_type=jnp.float32) + cross_bias
    crossed = x_zero * cross_pre + x_zero
    deep_pre = jnp.dot(x_low, deep_weight, preferred_element_type=jnp.float32) + deep_bias
    deep_act, gelu_back = jax.vjp(partial(jax.nn.gelu, approximate=True), deep_pre)
    logit = (
        jnp.sum(crossed * head_cross[None, :], axis=1)
        + jnp.sum(deep_act * head_deep[None, :], axis=1)
        + head_bias[0]
    )
    labels = clicked.astype(jnp.float32)
    loss_sum = jnp.sum(jax.nn.softplus(logit) - labels * logit)
    examples = batch_group * lax.axis_size("dp")
    scale = 1.0 / math.sqrt(examples)
    dlogit = (jax.nn.sigmoid(logit) - labels) * scale
    head_cross_grad = jnp.sum(dlogit[:, None] * crossed, axis=0)
    head_deep_grad = jnp.sum(dlogit[:, None] * deep_act, axis=0)
    head_bias_grad = jnp.sum(dlogit)[None]
    dcrossed = dlogit[:, None] * head_cross[None, :]
    ddeep_low = gelu_back(dlogit[:, None] * head_deep[None, :])[0].astype(jnp.bfloat16)
    dcross_low = (dcrossed * x_zero).astype(jnp.bfloat16)
    cross_weight_grad = contract_rows(x_low, dcross_low)
    cross_bias_grad = jnp.sum(dcross_low.astype(jnp.float32), axis=0)
    deep_weight_grad = contract_rows(x_low, ddeep_low)
    deep_bias_grad = jnp.sum(ddeep_low.astype(jnp.float32), axis=0)
    dx_zero = (
        dcrossed * (cross_pre + 1.0)
        + contract_cols(dcross_low, cross_weight)
        + contract_cols(ddeep_low, deep_weight)
    )
    dense_grad = dx_zero[:, cat_width:].T * present_mask
    demb_low = dx_zero[:, :cat_width].astype(jnp.bfloat16)
    piece = lax.all_gather(demb_low, "mp", axis=0, tiled=True)
    part_ids = lax.slice_in_dim(chosen, 0, piece.shape[0], axis=1) - base_row
    table_term = jnp.zeros((table_rows, cat_width), jnp.float32) + spread(
        part_ids, piece, table_rows
    )
    tables_grad = lax.psum_scatter(table_term, "dp", scatter_dimension=0, tiled=True)
    totals = lax.psum(
        (
            loss_sum,
            cross_weight_grad,
            cross_bias_grad,
            deep_weight_grad,
            deep_bias_grad,
            head_cross_grad,
            head_deep_grad,
            head_bias_grad,
        ),
        ("dp", "mp"),
    )
    loss = totals[0] / examples
    return (
        logit,
        loss,
        dense_grad,
        tables_grad,
        totals[1],
        totals[2],
        totals[3],
        totals[4],
        totals[5],
        totals[6],
        totals[7],
    )


def solution(mesh):
    placed = (
        P(None, "dp"),
        P(None, "dp"),
        P(None, ("dp", "mp")),
        P(None, ("dp", "mp")),
        P(("dp", "mp")),
        P("mp", None),
        P(),
        P(),
        P(),
        P(),
        P(),
        P(),
        P(),
    )
    return jax.shard_map(
        body,
        mesh=mesh,
        in_specs=placed,
        out_specs=(
            P(("dp", "mp")),
            P(),
            P(None, ("dp", "mp")),
            P(("mp", "dp"), None),
            P(),
            P(),
            P(),
            P(),
            P(),
            P(),
            P(),
        ),
        check_vma=False,
    )
```

profile of v0, /device:TPU:0, one launch (start us, length us, event | category | flops | bytes accessed | tf_op | source)
XLA Modules:
  0.0 811.7 jit_solution(17318757779317233819)
XLA Ops:
  9.5 6.8 fusion.109
  16.4 6.0 fusion.110
  22.4 6.5 fusion.108
  28.9 6.5 fusion.107
  35.3 6.5 fusion.106
  41.8 6.5 fusion.105
  48.3 6.4 fusion.104
  54.7 6.4 fusion.128
  61.1 6.5 fusion.129
  67.6 6.5 fusion.127
  74.1 6.5 fusion.126
  80.6 6.5 fusion.125
  87.0 6.5 fusion.124
  93.5 6.8 fusion.123
  100.3 6.5 fusion.122
  106.8 6.5 fusion.121
  113.3 6.4 fusion.120
  119.7 6.5 fusion.119
  126.2 6.5 fusion.118
  132.7 6.5 fusion.117
  139.1 6.5 fusion.116
  145.6 6.5 fusion.115
  152.1 6.5 fusion.114
  158.6 6.5 fusion.113
  165.0 6.4 fusion.112
  171.4 6.5 fusion.111
  177.9 107.6 %concatenate.10 = bf16[6144,1014]{0,1:T(8,128)(2,1)} concatenate(bf16[6144,39]{0,1:T(8,128)(2,1)} %fusion.104, bf16[6144,39]{0,1:T(8,128)(2,1)} %fusion.105, bf16[6144,39]{0,1:T(8,128)(2,1)} %fusion.106, bf16[6144,39]{0,1:T(8,128)(2,1)} %fusion.107, bf16[6144,39]{0,1:T(8,128)(2,1)} %fusion.108, bf16[6144,39]{0,1:T(8,128)(2,1)S(1)} %fusion.109, bf16[6144,39]{0,1:T(8,128)(2,1)S(1)} %fusion.110, ...), dimensions={1} | concatenate | bytes 24920064 | tf_op jit(solution)/shard_map/concatenate | solution.py:24
  286.5 100.3 %reduce-scatter.3.cloned.1.call-done = bf16[1536,1014]{0,1:T(8,128)(2,1)} async-done(((bf16[6144,1014]{0,1:T(8,128)(2,1)}), bf16[1536,1014]{0,1:T(8,128)(2,1)}) %reduce-scatter.3.cloned.1.call-update) | async-done | bytes 3115024 | tf_op jit(solution)/shard_map/reduce_scatter | solution.py:79
  389.8 8.4 %multiply_reduce_fusion.3 = (f32[1536]{0:T(1024)S(1)}, f32[1536,1024]{1,0:T(8,128)}) fusion(f32[1024]{0:T(1024)S(1)} %copy-done.56, f32[1024]{0:T(1024)S(1)} %copy-done.57, bf16[1027,1024]{1,0:T(8,128)(2,1)S(1)} %copy-done.59, f32[1536,13]{0,1:T(8,128)S(1)} %multiply_bitcast_fusion, f32[1536,1014]{0,1:T(8,128)S(1)} %convert_element_type.16), kind=kOutput, calls=%fused_computation.183 | convolution fusion | flops 3254272512 | bytes 14718976 | tf_op jit(solution)/shard_map/dot_general | solution.py:87
  398.2 7.9 multiply_reduce_fusion.1
  406.7 8.3 %convert_reduce_fusion.1 = (f32[1024]{0:T(1024)S(1)}, bf16[1536,1024]{1,0:T(8,128)(2,1)S(1)}, f32[1024]{0:T(1024)}) fusion(f32[1536,1024]{1,0:T(8,128)} %get-tuple-element.57, f32[1024]{0:T(1024)S(1)} %copy-done.57, f32[1024]{0:T(1024)S(1)} %copy-done.56, f32[1536]{0:T(1024)S(1)} %get-tuple-element.20), kind=kLoop, calls=%fused_computation.182 | loop fusion | flops 42465280 | bytes 9459712 | tf_op jit(solution)/shard_map/reduce_sum | solution.py:108
  418.0 4.8 convolution_add_fusion.1
  431.1 9.6 %fusion.202 = f32[1027,1024]{1,0:T(8,128)} fusion(bf16[1536,1024]{1,0:T(8,128)(2,1)} %copy-done.6, f32[1536,13]{0,1:T(8,128)S(1)} %multiply_bitcast_fusion, f32[1536,1014]{0,1:T(8,128)} %copy-done.2), kind=kOutput, calls=%fused_computation.251 | convolution fusion | flops 3236972544 | bytes 13662208 | tf_op jit(solution)/shard_map/dot_general | solution.py:46
  440.7 10.2 %fusion.204 = f32[1027,1027]{1,0:T(8,128)} fusion(bf16[1536,1027]{0,1:T(8,128)(2,1)S(1)} %copy-done.5, f32[1536,13]{0,1:T(8,128)S(1)} %multiply_bitcast_fusion, f32[1536,1014]{0,1:T(8,128)} %copy-done.2), kind=kOutput, calls=%fused_computation.252 | convolution fusion | flops 3246437376 | bytes 13683748 | tf_op jit(solution)/shard_map/dot_general | solution.py:46
  451.2 61.6 %all-gather.2.cloned.1.call-done = bf16[6144,1014]{0,1:T(8,128)(2,1)} async-done(((bf16[1536,1014]{0,1:T(8,128)(2,1)}), bf16[6144,1014]{0,1:T(8,128)(2,1)}) %all-gather.2.cloned.1.call-update) | async-done | bytes 12460048 | tf_op jit(solution)/shard_map/all_gather | solution.py:116
  512.8 5.1 fusion.2
  517.9 5.0 fusion.4
  591.6 4.6 fusion.14
  596.2 4.6 fusion.30
  600.8 4.8 fusion.46
  605.6 4.6 fusion
  610.3 4.6 fusion.16
  614.9 4.8 fusion.32
  619.7 4.6 fusion.48
  624.3 36.7 %concatenate.12 = f32[1024,1014]{0,1:T(8,128)} concatenate(f32[1024,39]{0,1:T(8,128)S(1)} %fusion.50, f32[1024,39]{0,1:T(8,128)} %fusion.48, f32[1024,39]{0,1:T(8,128)} %fusion.46, f32[1024,39]{0,1:T(8,128)S(1)} %fusion.44, f32[1024,39]{0,1:T(8,128)S(1)} %fusion.42, f32[1024,39]{0,1:T(8,128)S(1)} %fusion.40, f32[1024,39]{0,1:T(8,128)S(1)} %fusion.38, f32[1024,39]{0,1:T(8,128)S(1)} %fusion.36, ...), dimensions={1} | concatenate | bytes 8306688 | tf_op jit(solution)/shard_map/concatenate | solution.py:42
  661.6 41.2 %all-reduce = (f32[]{:T(128)}, f32[1027]{0:T(1024)}, f32[1024]{0:T(1024)}, f32[1027]{0:T(1024)}, f32[1024]{0:T(1024)}, /*index=5*/f32[1]{0:T(128)}) all-reduce(f32[]{:T(128)} %fusion.196, f32[1027]{0:T(1024)S(1)} %get-tuple-element.24, f32[1024]{0:T(1024)S(1)} %get-tuple-element.22, ...), channel_id=1, replica_groups=mesh['dp'=8,'mp'=4] {'dp','mp'}, use_global_device_ids=true, to_apply=%region_4.5 | all-reduce | flops 4104 | bytes 32832 | tf_op jit(solution)/shard_map/psum | solution.py:122
  707.3 89.2 %reduce-scatter.5.cloned.1.call-done = f32[128,1014]{0,1:T(8,128)} async-done(((f32[1024,1014]{0,1:T(8,128)}), f32[128,1014]{0,1:T(8,128)}) %reduce-scatter.5.cloned.1.call-update) | async-done | bytes 519184 | tf_op jit(solution)/shard_map/reduce_scatter | solution.py:121
  796.5 5.1 copy.27
  (167 shorter events, 91.8 us)
Async XLA Ops:
  7.2 391.0 %copy-start = (bf16[1027,1027]{1,0:T(8,128)(2,1)S(1)}, bf16[1027,1027]{1,0:T(8,128)(2,1)}, u32[]{:S(2)}) copy-start(bf16[1027,1027]{1,0:T(8,128)(2,1)} %param.19) | copy-start | bytes 6328378
  7.2 379.6 %reduce-scatter.3.cloned.1.call-start = ((), (), s32[]{:S(2)}) async-start(), calls=%async_computation.2 | async-start | bytes 15605760 | tf_op jit(solution)/shard_map/reduce_scatter | solution.py:79
  7.2 9.2 %copy-start.60 = (bf16[1024,1014]{0,1:T(8,128)(2,1)S(1)}, bf16[1024,1014]{0,1:T(8,128)(2,1)}, u32[]{:S(2)}) copy-start(bf16[1024,1014]{0,1:T(8,128)(2,1)} %param.18) | copy-start | bytes 6230020
  9.0 13.4 %copy-start.22 = (s32[1,6144]{1,0:T(1,128)}, s32[1,6144]{1,0:T(1,128)S(1)}, u32[]{:S(2)}) copy-start(s32[1,6144]{1,0:T(1,128)S(1)} %get-tuple-element.48) | copy-start | bytes 73732
  9.0 13.4 %copy-start.24 = (s32[1,6144]{1,0:T(1,128)}, s32[1,6144]{1,0:T(1,128)S(1)}, u32[]{:S(2)}) copy-start(s32[1,6144]{1,0:T(1,128)S(1)} %get-tuple-element.47) | copy-start | bytes 73732
  9.0 13.4 %copy-start.20 = (s32[1,6144]{1,0:T(1,128)}, s32[1,6144]{1,0:T(1,128)S(1)}, u32[]{:S(2)}) copy-start(s32[1,6144]{1,0:T(1,128)S(1)} %get-tuple-element.49) | copy-start | bytes 73732
  9.0 19.8 %copy-start.18 = (s32[1,6144]{1,0:T(1,128)}, s32[1,6144]{1,0:T(1,128)S(1)}, u32[]{:S(2)}) copy-start(s32[1,6144]{1,0:T(1,128)S(1)} %get-tuple-element.50) | copy-start | bytes 73732
  9.0 26.3 %copy-start.14 = (s32[1,6144]{1,0:T(1,128)}, s32[1,6144]{1,0:T(1,128)S(1)}, u32[]{:S(2)}) copy-start(s32[1,6144]{1,0:T(1,128)S(1)} %get-tuple-element.51) | copy-start | bytes 73732
  9.1 32.8 %copy-start.12 = (s32[1,6144]{1,0:T(1,128)}, s32[1,6144]{1,0:T(1,128)S(1)}, u32[]{:S(2)}) copy-start(s32[1,6144]{1,0:T(1,128)S(1)} %get-tuple-element.52) | copy-start | bytes 73732
  9.1 39.2 %copy-start.16 = (s32[1,6144]{1,0:T(1,128)}, s32[1,6144]{1,0:T(1,128)S(1)}, u32[]{:S(2)}) copy-start(s32[1,6144]{1,0:T(1,128)S(1)} %get-tuple-element.53) | copy-start | bytes 73732
  9.4 45.3 %copy-start.52 = (s32[1,6144]{1,0:T(1,128)}, s32[1,6144]{1,0:T(1,128)S(1)}, u32[]{:S(2)}) copy-start(s32[1,6144]{1,0:T(1,128)S(1)} %get-tuple-element.29) | copy-start | bytes 73732
  9.4 51.7 %copy-start.28 = (s32[1,6144]{1,0:T(1,128)}, s32[1,6144]{1,0:T(1,128)S(1)}, u32[]{:S(2)}) copy-start(s32[1,6144]{1,0:T(1,128)S(1)} %get-tuple-element.28) | copy-start | bytes 73732
  9.4 58.2 %copy-start.50 = (s32[1,6144]{1,0:T(1,128)}, s32[1,6144]{1,0:T(1,128)S(1)}, u32[]{:S(2)}) copy-start(s32[1,6144]{1,0:T(1,128)S(1)} %get-tuple-element.30) | copy-start | bytes 73732
  9.4 64.6 %copy-start.48 = (s32[1,6144]{1,0:T(1,128)}, s32[1,6144]{1,0:T(1,128)S(1)}, u32[]{:S(2)}) copy-start(s32[1,6144]{1,0:T(1,128)S(1)} %get-tuple-element.31) | copy-start | bytes 73732
  9.4 71.1 %copy-start.46 = (s32[1,6144]{1,0:T(1,128)}, s32[1,6144]{1,0:T(1,128)S(1)}, u32[]{:S(2)}) copy-start(s32[1,6144]{1,0:T(1,128)S(1)} %get-tuple-element.32) | copy-start | bytes 73732
  9.5 77.6 %copy-start.44 = (s32[1,6144]{1,0:T(1,128)}, s32[1,6144]{1,0:T(1,128)S(1)}, u32[]{:S(2)}) copy-start(s32[1,6144]{1,0:T(1,128)S(1)} %get-tuple-element.33) | copy-start | bytes 73732
  9.5 84.1 %copy-start.42 = (s32[1,6144]{1,0:T(1,128)}, s32[1,6144]{1,0:T(1,128)S(1)}, u32[]{:S(2)}) copy-start(s32[1,6144]{1,0:T(1,128)S(1)} %get-tuple-element.34) | copy-start | bytes 73732
  9.5 90.9 %copy-start.30 = (s32[1,6144]{1,0:T(1,128)}, s32[1,6144]{1,0:T(1,128)S(1)}, u32[]{:S(2)}) copy-start(s32[1,6144]{1,0:T(1,128)S(1)} %get-tuple-element.35) | copy-start | bytes 73732
  9.5 97.3 %copy-start.26 = (s32[1,6144]{1,0:T(1,128)}, s32[1,6144]{1,0:T(1,128)S(1)}, u32[]{:S(2)}) copy-start(s32[1,6144]{1,0:T(1,128)S(1)} %get-tuple-element.36) | copy-start | bytes 73732
  9.5 103.8 %copy-start.40 = (s32[1,6144]{1,0:T(1,128)}, s32[1,6144]{1,0:T(1,128)S(1)}, u32[]{:S(2)}) copy-start(s32[1,6144]{1,0:T(1,128)S(1)} %get-tuple-element.37) | copy-start | bytes 73732
  9.5 110.2 %copy-start.38 = (s32[1,6144]{1,0:T(1,128)}, s32[1,6144]{1,0:T(1,128)S(1)}, u32[]{:S(2)}) copy-start(s32[1,6144]{1,0:T(1,128)S(1)} %get-tuple-element.38) | copy-start | bytes 73732
  9.5 116.7 %copy-start.36 = (s32[1,6144]{1,0:T(1,128)}, s32[1,6144]{1,0:T(1,128)S(1)}, u32[]{:S(2)}) copy-start(s32[1,6144]{1,0:T(1,128)S(1)} %get-tuple-element.39) | copy-start | bytes 73732
  9.5 123.1 %copy-start.34 = (s32[1,6144]{1,0:T(1,128)}, s32[1,6144]{1,0:T(1,128)S(1)}, u32[]{:S(2)}) copy-start(s32[1,6144]{1,0:T(1,128)S(1)} %get-tuple-element.40) | copy-start | bytes 73732
  9.5 129.6 %copy-start.32 = (s32[1,6144]{1,0:T(1,128)}, s32[1,6144]{1,0:T(1,128)S(1)}, u32[]{:S(2)}) copy-start(s32[1,6144]{1,0:T(1,128)S(1)} %get-tuple-element.41) | copy-start | bytes 73732
  285.5 104.2 %copy-start.56 = (f32[1024]{0:T(1024)S(1)}, f32[1024]{0:T(1024)}, u32[]{:S(2)}) copy-start(f32[1024]{0:T(1024)} %param.24) | copy-start | bytes 12292
  285.6 104.2 %copy-start.57 = (f32[1024]{0:T(1024)S(1)}, f32[1024]{0:T(1024)}, u32[]{:S(2)}) copy-start(f32[1024]{0:T(1024)} %param.22) | copy-start | bytes 12292
  285.6 227.2 %all-gather.2.cloned.1.call-start = ((), (), s32[]{:S(2)}) async-start(), calls=%async_computation.3 | async-start | bytes 15605760 | tf_op jit(solution)/shard_map/all_gather | solution.py:116
  389.7 25.3 %copy-start.2 = (f32[1536,1014]{0,1:T(8,128)}, f32[1536,1014]{0,1:T(8,128)S(1)}, u32[]{:S(2)}) copy-start(f32[1536,1014]{0,1:T(8,128)S(1)} %convert_element_type.16) | copy-start | bytes 18690052
  389.7 8.4 %copy-start.55 = (f32[1027]{0:T(1024)S(1)}, f32[1027]{0:T(1024)}, u32[]{:S(2)}) copy-start(f32[1027]{0:T(1024)} %param.23) | copy-start | bytes 12328
  389.8 8.4 %copy-start.61 = (f32[1027]{0:T(1024)S(1)}, f32[1027]{0:T(1024)}, u32[]{:S(2)}) copy-start(f32[1027]{0:T(1024)} %param.20) | copy-start | bytes 12328
  398.2 8.0 copy-start.10
  406.1 9.0 %copy-start.3 = (f32[1536,1027]{0,1:T(8,128)S(1)}, f32[1536,1027]{0,1:T(8,128)}, u32[]{:S(2)}) copy-start(f32[1536,1027]{0,1:T(8,128)} %get-tuple-element.55) | copy-start | bytes 18929668
  406.7 254.3 %copy-start.11 = (f32[1536]{0:T(1024)}, f32[1536]{0:T(1024)S(1)}, u32[]{:S(2)}) copy-start(f32[1536]{0:T(1024)S(1)} %get-tuple-element.58) | copy-start | bytes 18436
  415.1 7.8 copy-start.6
  418.0 4.9 copy-start.4
  431.1 276.2 %all-reduce.4.cloned.1.call-start = ((), (), s32[]{:S(2)}) async-start(), calls=%async_computation.5 | async-start | bytes 17965056 | tf_op jit(solution)/shard_map/psum | solution.py:122
  431.1 9.6 %copy-start.5 = (bf16[1536,1027]{0,1:T(8,128)(2,1)S(1)}, bf16[1536,1027]{0,1:T(8,128)(2,1)}, u32[]{:S(2)}) copy-start(bf16[1536,1027]{0,1:T(8,128)(2,1)} %copy-done.4) | copy-start | bytes 9464836
  450.9 61.8 %copy-start.53 = (s32[1,6144]{1,0:T(1,128)S(1)}, s32[1,6144]{1,0:T(1,128)}, u32[]{:S(2)}) copy-start(s32[1,6144]{1,0:T(1,128)} %copy-done.52) | copy-start | bytes 73732
  451.0 66.9 %copy-start.51 = (s32[1,6144]{1,0:T(1,128)S(1)}, s32[1,6144]{1,0:T(1,128)}, u32[]{:S(2)}) copy-start(s32[1,6144]{1,0:T(1,128)} %copy-done.50) | copy-start | bytes 73732
  451.0 345.5 %reduce-scatter.5.cloned.1.call-start = ((), (), s32[]{:S(2)}) async-start(), calls=%async_computation.4 | async-start | bytes 4681728 | tf_op jit(solution)/shard_map/reduce_scatter | solution.py:121
  512.8 10.1 %copy-start.58 = (bf16[6144,1014]{0,1:T(8,128)(2,1)S(1)}, bf16[6144,1014]{0,1:T(8,128)(2,1)}, u32[]{:S(2)}) copy-start(bf16[6144,1014]{0,1:T(8,128)(2,1)} %all-gather.2.cloned.1.call-done) | copy-start | bytes 37380100
  517.9 5.0 copy-start.49
  600.8 4.8 copy-start.29
  614.9 4.9 copy-start.13
  624.3 37.3 %copy-start.54 = (f32[1024]{0:T(1024)S(1)}, f32[1024]{0:T(1024)}, u32[]{:S(2)}) copy-start(f32[1024]{0:T(1024)} %get-tuple-element.27) | copy-start | bytes 12292
  707.3 94.3 %slice-start = ((s8[4227072]{0:T(1024)(128)(4,1)}), s8[32768]{0:T(1024)(128)(4,1)S(1)}, s32[]{:S(2)}) async-start(s8[4227072]{0:T(1024)(128)(4,1)} %bitcast.43), calls=%async_computation.6 | async-start | bytes 65536
  796.5 5.1 slice-start.1
  796.5 7.1 copy-start.1
  (20 other events, 73.2 us)
Sparse Core Ops, SparseCore 0:
  285.7 101.1 reduce-scatter.2
  431.2 81.5 all-gather.1
  519.3 187.9 all-reduce.3
  711.1 85.2 reduce-scatter.4
where the time goes:
time: 826 us; the launch traced here: 812 us
  matrix products  323 us (39%)
  waiting for transfers between devices  253 us (31%)
  local copies, waits for them, and re-layouts  157 us (19%)
  blocking collectives  41.2 us (5%)
  other arithmetic  18.6 us (2%)
  between operations  17.9 us (2%)
    dot_general x26, matrix products, lookup(): jnp.dot(onehot, piece[:, field * emb_width:(field + 1) * emb_width], pref...  168 us
    dot_general x26, matrix products, spread(): lax.dot_general(onehot, grads[:, field * emb_width:(field + 1) * emb_widt...  111 us
    concatenate x1, local copies, waits for them, and re-layouts, lookup(): return jnp.concatenate(blocks, axis=1)  108 us
    reduce_scatter x1, waiting for transfers between devices, body(): lax.psum_scatter(lookup(part_ids, tables).astype(jnp.bfloat16), 'mp', sca...  100 us
    reduce_scatter x1, waiting for transfers between devices, body(): lax.psum_scatter(table_term, 'dp', scatter_dimension=0, tiled=True)  89.2 us
    all_gather x1, waiting for transfers between devices, body(): piece = lax.all_gather(demb_low, 'mp', axis=0, tiled=True)  61.6 us
    psum x1, blocking collectives, body(): lax.psum((loss_sum, cross_weight_grad, cross_bias_grad, deep_weight_grad,...  41.2 us
    concatenate x1, local copies, waits for them, and re-layouts, spread(): return jnp.concatenate(blocks, axis=1)  36.7 us
  transfers between devices with their start and end apart: 4, of which 4 were waited for; matrix products, arithmetic and copies ran while one was open for 21% of the time, Pallas kernels for 0%

commit v1 on v0

v1 whole, which is shorter than its diff:
```python
import math

import jax
import jax.numpy as jnp
from jax import lax
from jax.experimental import pallas as pl
from jax.experimental.pallas import tpu as pltpu
from jax.sharding import PartitionSpec as P

BF16, F32, F16 = jnp.bfloat16, jnp.float32, jnp.float16
HI = 256
FRONT = 8
PAD = 40
TILE = 256
TOP = 32768.0
LIMIT = 60 * 1024 * 1024
GELU_S = math.sqrt(2.0 / math.pi)
GELU_C = 0.044715


def params(**more):
    return pltpu.CompilerParams(vmem_limit_bytes=LIMIT, **more)


def cost(flops, moved):
    return pl.CostEstimate(flops=int(flops), bytes_accessed=int(moved), transcendentals=0)


def ceil_to(value, unit):
    return -(-value // unit) * unit


def dot_nn(left, right):
    return jnp.dot(left, right, preferred_element_type=F32)


def dot_nt(left, right, precision=None):
    return lax.dot_general(
        left, right, (((1,), (1,)), ((), ())), preferred_element_type=F32, precision=precision
    )


def onehot_rows(place, width):
    rows = lax.broadcasted_iota(jnp.int16, (HI, width), 0)
    return jnp.where(rows == place.astype(jnp.int16), jnp.ones((), BF16), jnp.zeros((), BF16))


def lookup_kernel(emb, blocks, hi_ref, lo_ref, *refs):
    sources, out_ref, flat, packed = refs[:4], refs[4], refs[5], refs[6]
    n_fields, examples = hi_ref.shape
    rows = emb * n_fields
    for s, source in enumerate(sources):
        flat[s, 0:rows, :] = source[...].astype(F32)
    for f in range(n_fields):
        for s in range(4):
            for b in range(blocks):
                piece = flat[s, emb * f : emb * f + PAD, b * HI : (b + 1) * HI]
                at = (s * blocks + b) * PAD
                packed[f, at : at + PAD, :] = piece.astype(BF16)

    def step(t, carry):
        at = pl.multiple_of(t * TILE, TILE)
        for f in range(n_fields):
            place = hi_ref[f : f + 1, pl.ds(at, TILE)]
            block = lo_ref[f : f + 1, pl.ds(at, TILE)]
            found = dot_nn(packed[f], onehot_rows(place, TILE))
            acc = found[0:PAD]
            for b in range(1, 4 * blocks):
                acc = jnp.where(block == b, found[b * PAD : (b + 1) * PAD], acc)
            out_ref[f, :, pl.ds(at, TILE)] = acc
        return carry

    lax.fori_loop(0, examples // TILE, step, 0)


def lookup(hi, lo, sources, emb):
    n_fields, examples = hi.shape
    rows, width = sources[0].shape
    blocks = width // HI
    n_rows = 4 * blocks * PAD
    return pl.pallas_call(
        lambda *refs: lookup_kernel(emb, blocks, *refs),
        out_shape=jax.ShapeDtypeStruct((n_fields, PAD, examples), F32),
        scratch_shapes=[
            pltpu.VMEM((4, ceil_to(rows, 8) + 8, width), F32),
            pltpu.VMEM((n_fields, n_rows, HI), BF16),
        ],
        compiler_params=params(),
        cost_estimate=cost(2 * n_fields * n_rows * HI * examples, 4 * n_fields * PAD * examples),
        name="lookup",
    )(hi, lo, *sources)


def wide(column, width):
    return jnp.concatenate([column] * (width // 128), axis=1)


def fold(values):
    total = values[:, 0:128]
    for at in range(128, values.shape[1], 128):
        total = total + values[:, at : at + 128]
    return total


def layers_kernel(sizes, scale, *refs):
    fields, emb, dense, n_chunks = sizes
    chunks = refs[:n_chunks]
    (dv_ref, dm_ref, lab_ref, wt_ref, w_ref, dwt_ref, dw_ref, cb_ref, db_ref, hc_ref, hd_ref, hb_ref) = refs[
        n_chunks : n_chunks + 12
    ]
    (logit_ref, xa_ref, dc_ref, dd_ref, demb_ref, dg_ref, hca_ref, hda_ref, sc_ref) = refs[
        n_chunks + 12 : n_chunks + 21
    ]
    x_ref, cp_ref, dp_ref = refs[n_chunks + 21 :]
    rows, width = x_ref.shape
    cat = fields * emb
    full = cat + dense
    hidden = dp_ref.shape[0]
    step = 128
    cuts = [(a, min(a + step, rows)) for a in range(0, rows, step)]
    hid_cuts = [(a, min(a + step, hidden)) for a in range(0, hidden, step)]

    @pl.when(pl.program_id(0) == 0)
    def _():
        hca_ref[...] = jnp.zeros_like(hca_ref)
        hda_ref[...] = jnp.zeros_like(hda_ref)
        sc_ref[...] = jnp.zeros_like(sc_ref)

    f = 0
    for chunk in chunks:
        for k in range(chunk.shape[0]):
            x_ref[emb * f : emb * f + PAD, :] = chunk[k]
            f += 1
    x_ref[cat:full, :] = dv_ref[...] * dm_ref[...].astype(F32)
    x_ref[full:rows, :] = jnp.zeros((rows - full, width), F32)
    x_low = x_ref[...].astype(BF16)
    tail = xa_ref.shape[0] - (cat // 16) * 16
    base = xa_ref.shape[0] - tail
    xa_ref[0:base, :] = x_low[0:base]
    last = jnp.concatenate([x_ref[base:rows, :], jnp.zeros((base + tail - rows, width), F32)], axis=0)
    index = lax.broadcasted_iota(jnp.int32, (tail, width), 0) + base
    xa_ref[base:, :] = jnp.where(index == full, 1.0, last).astype(BF16)

    cp_ref[...] = dot_nn(wt_ref[...], x_low)
    dp_ref[...] = dot_nn(dwt_ref[...], x_low)
    logit = jnp.zeros((8, width), F32)
    for a, b in cuts:
        x = x_ref[a:b, :]
        cp = cp_ref[a:b, :] + wide(cb_ref[a:b, :], width)
        cp_ref[a:b, :] = cp
        term = (x * cp + x) * wide(hc_ref[a:b, :], width)
        for r in range(0, b - a, 8):
            logit = logit + term[r : r + 8]
    for a, b in hid_cuts:
        v = dp_ref[a:b, :] + wide(db_ref[a:b, :], width)
        dp_ref[a:b, :] = v
        act = 0.5 * v * (1.0 + jnp.tanh(GELU_S * (v + GELU_C * v * v * v)))
        term = act * wide(hd_ref[a:b, :], width)
        for r in range(0, b - a, 8):
            logit = logit + term[r : r + 8]
    logit = jnp.sum(logit, axis=0, keepdims=True) + hb_ref[0:1, 0:1]
    logit_ref[...] = logit
    labels = lab_ref[...].astype(F32)
    small = jnp.exp(-jnp.abs(logit))
    loss = jnp.maximum(logit, 0.0) + jnp.log1p(small) - labels * logit
    sig = jnp.where(logit >= 0.0, 1.0, small) / (1.0 + small)
    dlogit = (sig - labels) * scale
    sc_ref[0:1, :] += fold(loss)
    sc_ref[1:2, :] += fold(dlogit)

    for a, b in cuts:
        x = x_ref[a:b, :]
        cp = cp_ref[a:b, :]
        hca_ref[a:b, :] += fold(dlogit * (x * cp + x))
        dcrossed = dlogit * wide(hc_ref[a:b, :], width)
        dc_ref[a:b, :] = (dcrossed * x).astype(BF16)
        cp_ref[a:b, :] = dcrossed * (cp + 1.0)
    if dc_ref.shape[0] > rows:
        dc_ref[rows:, :] = jnp.zeros((dc_ref.shape[0] - rows, width), BF16)
    for a, b in hid_cuts:
        v = dp_ref[a:b, :]
        t = jnp.tanh(GELU_S * (v + GELU_C * v * v * v))
        half = 0.5 * (1.0 + t)
        hda_ref[a:b, :] += fold(dlogit * (v * half))
        slope = half + 0.5 * v * (1.0 - t * t) * (GELU_S * (1.0 + 3.0 * GELU_C * v * v))
        dd_ref[a:b, :] = (dlogit * wide(hd_ref[a:b, :], width) * slope).astype(BF16)
    x_ref[...] = (
        cp_ref[...] + dot_nn(w_ref[...], dc_ref[0:rows, :]) + dot_nn(dw_ref[...], dd_ref[...])
    )
    for f in range(fields):
        demb_ref[f] = x_ref[emb * f : emb * f + PAD, :].astype(BF16)
    dg_ref[...] = x_ref[cat:full, :] * dm_ref[...].astype(F32)


def layers(chunks, dense_values, dense_present, labels, weights, columns, emb, scale):
    wt, w, dwt, dw = weights
    fields = sum(c.shape[0] for c in chunks)
    dense, examples = dense_values.shape
    rows, hidden = w.shape[0], dw.shape[1]
    tall = ceil_to(rows, 16)
    column = lambda r: pl.BlockSpec((r, TILE), lambda t: (0, t))
    whole = lambda a: pl.BlockSpec(a.shape, lambda t: (0,) * a.ndim, pipeline_mode=pl.Buffered(1))
    kept = lambda r: pl.BlockSpec((r, 128), lambda t: (0, 0))
    shape = jax.ShapeDtypeStruct
    return pl.pallas_call(
        lambda *refs: layers_kernel((fields, emb, dense, len(chunks)), scale, *refs),
        grid=(examples // TILE,),
        in_specs=[pl.BlockSpec((c.shape[0], PAD, TILE), lambda t: (0, 0, t)) for c in chunks]
        + [column(dense), column(dense), column(1)]
        + [whole(a) for a in (wt, w, dwt, dw, *columns)],
        out_specs=[
            column(1),
            column(tall),
            column(tall),
            column(hidden),
            pl.BlockSpec((fields, PAD, TILE), lambda t: (0, 0, t)),
            column(dense),
            kept(rows),
            kept(hidden),
            kept(8),
        ],
        out_shape=[
            shape((1, examples), F32),
            shape((tall, examples), BF16),
            shape((tall, examples), BF16),
            shape((hidden, examples), BF16),
            shape((fields, PAD, examples), BF16),
            shape((dense, examples), F32),
            shape((rows, 128), F32),
            shape((hidden, 128), F32),
            shape((8, 128), F32),
        ],
        scratch_shapes=[
            pltpu.VMEM((rows, TILE), F32),
            pltpu.VMEM((rows, TILE), F32),
            pltpu.VMEM((hidden, TILE), F32),
        ],
        compiler_params=params(),
        cost_estimate=cost(2 * examples * rows * (2 * rows + 2 * hidden), 9 * 2**20 + 20 * rows * examples),
        name="layers",
    )(*chunks, dense_values, dense_present, labels, wt, w, dwt, dw, *columns)


def weight_kernel(rows, full, examples_all, xa_ref, xb_ref, dc_ref, dct_ref, dd_ref, hc_ref, hct_ref, hd_ref, sc_ref, out_ref, top_ref):
    quarter = out_ref.shape[3] - FRONT
    core = pl.program_id(0) // (pl.num_programs(0) // 2)
    x = xa_ref[0:rows, :]
    deep = dot_nt(x, dd_ref[...])
    cross = dot_nt(x, dc_ref[...])
    tail = dct_ref[...]
    over = dot_nt(tail, xb_ref[...])[0:8]
    corner = dot_nt(tail, xa_ref[xa_ref.shape[0] - 16 :, :])
    ones = jnp.ones((8, 128), F32)
    total = lambda ref: dot_nt(ones, ref[...], lax.Precision.HIGHEST)
    row = lax.broadcasted_iota(jnp.int32, (8, TILE), 0)
    first = pl.program_id(0) == 0
    heads = jnp.where(row == 0, total(hc_ref), jnp.where(row == 1, total(hd_ref), 0.0))
    spare = jnp.concatenate([corner[0:8], jnp.zeros((8, TILE - 16), F32)], axis=1)
    spare = jnp.concatenate([jnp.zeros((2, TILE), F32), spare[0:3], jnp.zeros((3, TILE), F32)], axis=0)
    ends = total(hct_ref)
    ends = jnp.concatenate([ends, jnp.zeros((8, TILE - 8), F32)], axis=1)
    sums = jnp.sum(sc_ref[...], axis=1, keepdims=True)
    lane = lax.broadcasted_iota(jnp.int32, (8, TILE), 1)
    scalars = jnp.where(lane == 0, sums[0:1] / examples_all, jnp.where(lane == 1, sums[1:2], 0.0))
    small = spare + jnp.where(row == 5, ends, 0.0) + jnp.where(row == 6, scalars, 0.0)
    heads = heads + jnp.where(first, small, 0.0)
    parts = [(0, deep), (rows, cross), (2 * rows, over), (2 * rows + 8, heads)]
    top = jnp.zeros((8, TILE), F32)
    for base, part in parts:
        for r in range(0, part.shape[0], 8):
            top = jnp.maximum(top, jnp.abs(part[r : r + 8]))
    top = jnp.maximum(top[:, 0:128], top[:, 128:256])

    @pl.when(first)
    def _():
        top_ref[...] = top

    @pl.when(jnp.logical_not(first))
    def _():
        top_ref[...] = jnp.maximum(top_ref[...], top)

    for base, part in parts:
        at = 0
        while at < part.shape[0]:
            q, r = divmod(base + at, quarter)
            n = min(part.shape[0] - at, quarter - r)
            place = jnp.where(core == 0, (0, 2, 1, 3)[q], q)
            for h in range(2):
                out_ref[0, place, h, FRONT + r : FRONT + r + n, :] = part[at : at + n, h * 128 : (h + 1) * 128]
            at += n


def weight_grads(xa, dc, dd, hca, hda, sc, full, examples_all):
    tall, examples = xa.shape
    rows, hidden = hca.shape[0], hda.shape[0]
    quarter = ceil_to(2 * rows + 16, 32) // 4
    return pl.pallas_call(
        lambda *refs: weight_kernel(rows, full, examples_all, *refs),
        grid=(hidden // TILE,),
        in_specs=[
            pl.BlockSpec((tall, examples), lambda j: (0, 0), pipeline_mode=pl.Buffered(1)),
            pl.BlockSpec((TILE, examples), lambda j: (j, 0)),
            pl.BlockSpec((TILE, examples), lambda j: (j, 0)),
            pl.BlockSpec((16, examples), lambda j: (hidden // 16, 0)),
            pl.BlockSpec((TILE, examples), lambda j: (j, 0)),
            pl.BlockSpec((TILE, 128), lambda j: (j, 0)),
            pl.BlockSpec((8, 128), lambda j: (hidden // 8, 0)),
            pl.BlockSpec((TILE, 128), lambda j: (j, 0)),
            pl.BlockSpec((8, 128), lambda j: (0, 0)),
        ],
        out_specs=[
            pl.BlockSpec((1, 4, 2, FRONT + quarter, 128), lambda j: (j // 2, 0, j % 2, 0, 0)),
            pl.BlockSpec((8, 128), lambda j: (0, 0)),
        ],
        out_shape=[
            jax.ShapeDtypeStruct((2, 4, hidden // 256, FRONT + quarter, 128), F32),
            jax.ShapeDtypeStruct((8, 128), F32),
        ],
        compiler_params=params(),
        cost_estimate=cost(4 * examples * rows * hidden, 20 * rows * hidden),
        name="weight_grads",
    )(xa, xa, dc, dc, dd, hca, hca, hda, sc)


def spread_kernel(hi_ref, lo_ref, own_ref, sib_ref, out_ref, top_ref, sel, hot):
    n_blocks = out_ref.shape[0] * out_ref.shape[1]
    examples = own_ref.shape[2]
    for s, ref in enumerate((own_ref, sib_ref)):
        for at in range(0, examples, TILE):
            place = hi_ref[0, s : s + 1, at : at + TILE]
            block = lo_ref[0, s : s + 1, at : at + TILE]
            grads = ref[0, :, at : at + TILE].astype(F32)
            cols = slice(s * examples + at, s * examples + at + TILE)
            sel[:, cols] = jnp.concatenate(
                [jnp.where(block == b, grads, 0.0) for b in range(n_blocks)], axis=0
            ).astype(BF16)
            hot[:, cols] = onehot_rows(place, TILE)
    sums = dot_nt(sel[...], hot[...])
    top = jnp.zeros((8, HI), F32)
    for r in range(0, sums.shape[0], 8):
        top = jnp.maximum(top, jnp.abs(sums[r : r + 8]))
    top = jnp.maximum(top[:, 0:128], top[:, 128:256])

    @pl.when(pl.program_id(0) == 0)
    def _():
        top_ref[...] = top

    @pl.when(pl.program_id(0) != 0)
    def _():
        top_ref[...] = jnp.maximum(top_ref[...], top)

    for b in range(n_blocks):
        for h in range(2):
            out_ref[b // out_ref.shape[1], b % out_ref.shape[1], h] = sums[
                b * PAD : (b + 1) * PAD, h * 128 : (h + 1) * 128
            ]


def spread(hi, lo, own, sib, first, count, blocks):
    fields, _, examples = own.shape
    return pl.pallas_call(
        spread_kernel,
        grid=(count,),
        in_specs=[pl.BlockSpec((1, 2, examples), lambda f: (f + first, 0, 0))] * 2
        + [pl.BlockSpec((1, PAD, examples), lambda f: (f + first, 0, 0))] * 2,
        out_specs=[
            pl.BlockSpec((2, blocks, 2, PAD, 128), lambda f: (0, 0, 0, f, 0)),
            pl.BlockSpec((8, 128), lambda f: (0, 0)),
        ],
        out_shape=[
            jax.ShapeDtypeStruct((2, blocks, 2, count * PAD, 128), F32),
            jax.ShapeDtypeStruct((8, 128), F32),
        ],
        scratch_shapes=[
            pltpu.VMEM((2 * blocks * PAD, 2 * examples), BF16),
            pltpu.VMEM((HI, 2 * examples), BF16),
        ],
        compiler_params=params(),
        cost_estimate=cost(8 * count * blocks * PAD * HI * examples, 4 * count * PAD * 16 * 128 * blocks),
        name="spread",
    )(hi, lo, own, sib)


def flip(array, axis, bit):
    size = lax.axis_size(axis)
    return lax.ppermute(array, axis, [(i, i ^ (1 << bit)) for i in range(size)])


def bit_of(axis, bit):
    return (lax.axis_index(axis) >> bit) & 1


def crossed_pairs(stage, n_dp, n_mp):
    pairs = []
    for d in range(n_dp):
        for m in range(n_mp):
            along_dp = (m & 1) == stage
            to = (d ^ 1, m) if along_dp else (d, m ^ 2)
            pairs.append((d * n_mp + m, to[0] * n_mp + to[1]))
    return pairs


def crossed_flip(array, stage):
    return lax.ppermute(array, ("dp", "mp"), crossed_pairs(stage, lax.axis_size("dp"), lax.axis_size("mp")))


def crossed_bit(stage):
    return jnp.where(bit_of("mp", 0) == stage, bit_of("dp", 0), bit_of("mp", 1))


def exponent_of(top):
    top = jnp.maximum(jnp.max(top, axis=(0, 1), keepdims=True)[0], 1e-30)
    return jnp.broadcast_to(jnp.ceil(jnp.log2(top)) - 14.0, (128,))


def halve(acc, expo, mine, send, at):
    away = lax.dynamic_index_in_dim(acc, 1 - mine, 0, keepdims=False)
    kept = lax.dynamic_index_in_dim(acc, mine, 0, keepdims=False)
    row = lax.broadcasted_iota(jnp.int32, away.shape, away.ndim - 2)
    here = expo.reshape((1,) * (away.ndim - 1) + (128,))
    message = jnp.where(row == at, here, away * jnp.exp2(-here)).astype(F16)
    got = send(message)
    theirs = got[(0,) * (got.ndim - 2) + (at,)].astype(F32)
    acc = kept + got.astype(F32) * jnp.exp2(theirs).reshape(here.shape[: got.ndim])
    return acc, jnp.maximum(expo, theirs) + 1.0


def double(piece, mine, send):
    other = send(piece)
    low = mine == 0
    return jnp.stack([jnp.where(low, piece, other), jnp.where(low, other, piece)], axis=0)


def stages():
    return [
        (crossed_bit(0), lambda a: crossed_flip(a, 0)),
        (crossed_bit(1), lambda a: crossed_flip(a, 1)),
        (bit_of("dp", 1), lambda a: flip(a, "dp", 1)),
        (bit_of("dp", 2), lambda a: flip(a, "dp", 2)),
    ]


def assemble_kernel(rows, full, hidden, step_cols, in_ref, over_ref, cross_ref, deep_ref, vec_ref):
    t = pl.program_id(0)
    last = pl.num_programs(0) - 1
    core = t // (step_cols // 2)
    quarter = in_ref.shape[4] - FRONT
    parts = []
    for r in range(4):
        q = jnp.where(core == 0, (0, 2, 1, 3)[r], r)
        parts.append(in_ref[0, q // 2, q % 2, 0, FRONT:, :])
    every = jnp.concatenate(parts, axis=0)

    @pl.when(t < last)
    def _():
        deep_ref[...] = every[0:full]
        cross_ref[...] = every[rows : rows + full]
        vec_ref[0:1, :] = every[rows + full : rows + full + 1]
        vec_ref[1:2, :] = every[full : full + 1]
        vec_ref[2:4, :] = every[2 * rows + 8 : 2 * rows + 10]
        vec_ref[4:8, :] = every[2 * rows + 12 : 2 * rows + 16]

    @pl.when(t == last)
    def _():
        cross_ref[...] = over_ref[0:full, :]


def assemble(pieces, rows, full, hidden):
    cols = hidden // 128
    quarter = pieces.shape[4] - FRONT
    z = cols // 2
    spare = pieces[:, 1, 1, :, FRONT + quarter - 16 :, :].transpose(2, 0, 1, 3).reshape(16, hidden)
    extra = full - hidden
    over = jnp.concatenate([spare[0:8], jnp.zeros((8, 128), F32)], axis=1)[0:extra]
    over = lax.dynamic_update_slice(over, spare[10 : 10 + extra, 0 : rows - hidden], (0, hidden))[:, 0:rows]
    over = jnp.pad(over.T, ((0, 0), (0, 128 - extra)))
    return pl.pallas_call(
        lambda *refs: assemble_kernel(rows, full, hidden, cols, *refs),
        grid=(cols + 1,),
        in_specs=[
            pl.BlockSpec(
                (1, 2, 2, 1, FRONT + quarter, 128),
                lambda t: (jnp.minimum(t, cols - 1) // z, 0, 0, jnp.minimum(t, cols - 1) % z, 0, 0),
            ),
            pl.BlockSpec((rows, 128), lambda t: (0, 0)),
        ],
        out_specs=[
            pl.BlockSpec((full, 128), lambda t: (0, t)),
            pl.BlockSpec((full, 128), lambda t: (0, jnp.minimum(t, cols - 1))),
            pl.BlockSpec((8, 128), lambda t: (0, jnp.minimum(t, cols - 1))),
        ],
        out_shape=[
            jax.ShapeDtypeStruct((full, full), F32),
            jax.ShapeDtypeStruct((full, hidden), F32),
            jax.ShapeDtypeStruct((8, hidden), F32),
        ],
        compiler_params=params(),
        cost_estimate=cost(0, 16 * rows * hidden),
        name="assemble",
    )(pieces, over), over


def table_place(ids, table_rows, n_dp, core):
    upper = ids // (2 * table_rows)
    rest = ids % table_rows
    if n_dp == 8:
        piece = table_rows // n_dp
        at = rest // piece
        low = at % 2
        first = jnp.where(core == 0, low, upper)
        second = jnp.where(core == 0, upper, low)
        block = first * 4 + second * 2 + at // 4
        place = (at // 2) % 2 * piece + rest % piece
    else:
        block = upper * (table_rows // HI) + rest // HI
        place = rest % HI
    return place, jnp.where((ids // table_rows) % 2 == core, block, -1)


def body(
    field_ids,
    field_present,
    dense_values,
    dense_present,
    clicked,
    tables,
    cross_weight,
    cross_bias,
    deep_weight,
    deep_bias,
    head_cross,
    head_deep,
    head_bias,
):
    fields, batch_group = field_ids.shape
    table_rows, cat = tables.shape
    emb = cat // fields
    full, hidden = deep_weight.shape
    dense = full - cat
    n_dp, n_mp = lax.axis_size("dp"), lax.axis_size("mp")
    examples = batch_group // n_mp
    examples_all = batch_group * n_dp
    blocks = table_rows // HI
    rows = ceil_to(full + 1, 8)
    me = lax.axis_index("mp")
    core = me & 1

    columns = tables.T
    ends = [0, 8, 16, 24, fields]
    direct = [(d * n_mp + m, d * n_mp + (m ^ 2)) for d in range(n_dp) for m in range(n_mp) if (m & 1) == (d & 1)]
    relay = [(d * n_mp + m, (d ^ 1) * n_mp + m) for d in range(n_dp) for m in range(n_mp) if (m & 1) == (d & 1)]
    is_direct = core == bit_of("dp", 0)
    mine, near, far, far_near = [], [], [], []
    for a, b in zip(ends[:-1], ends[1:]):
        mine.append(columns[a * emb : b * emb])
    for part in mine:
        got = lax.ppermute(part, ("dp", "mp"), direct)
        far.append(jnp.where(is_direct, got, lax.ppermute(got, ("dp", "mp"), relay)))
    for part in mine:
        near.append(flip(part, "mp", 0))
    for part in far:
        far_near.append(flip(part, "mp", 0))

    chosen = jnp.where(field_present > 0, field_ids, 0)
    own_ids = lax.dynamic_slice_in_dim(chosen, me * examples, examples, 1)
    sib_ids = lax.dynamic_slice_in_dim(chosen, (me ^ 1) * examples, examples, 1)
    hi_own = own_ids & (HI - 1)
    lo_own = (own_ids // HI) ^ (me * blocks)
    pair_ids = jnp.stack([own_ids, sib_ids], axis=1)
    hi_pair, lo_pair = table_place(pair_ids, table_rows, n_dp, core)

    pad_in = rows - full
    w = jnp.pad(cross_weight, ((0, pad_in), (0, pad_in)))
    dw = jnp.pad(deep_weight, ((0, pad_in), (0, 0)))
    weights = (w.T, w, dw.T, dw)
    spread_out = lambda v, n: jnp.broadcast_to(jnp.pad(v, (0, n - v.shape[0]))[:, None], (n, 128))
    vectors = (
        spread_out(cross_bias, rows),
        spread_out(deep_bias, hidden),
        spread_out(head_cross, rows),
        spread_out(head_deep, hidden),
        spread_out(head_bias, 8),
    )

    chunks = []
    for k, (a, b) in enumerate(zip(ends[:-1], ends[1:])):
        ids = hi_own[a:b], lo_own[a:b]
        if chunks:
            ids, chunks[-1] = lax.optimization_barrier((ids, chunks[-1]))
        chunks.append(lookup(*ids, (mine[k], near[k], far[k], far_near[k]), emb))

    logit, xa, dc, dd, demb, dense_grad, hca, hda, sc = layers(
        chunks,
        dense_values,
        dense_present,
        clicked[None, :],
        weights,
        vectors,
        emb,
        1.0 / math.sqrt(examples_all),
    )
    demb_sib = flip(demb, "mp", 0)
    sums, top = weight_grads(xa, dc, dd, hca, hda, sc, full, examples_all)
    halves = [(0, 13), (13, fields)]
    table_parts = [spread(hi_pair, lo_pair, demb, demb_sib, a, b - a, blocks) for a, b in halves]

    if n_dp == 8:
        part, expo = halve(sums, exponent_of(top), core, lambda a: flip(a, "mp", 0), FRONT - 1)
        part = part.reshape(2, 2, *part.shape[1:])
        for k, (mine_bit, send) in enumerate(stages()):
            if k == 2:
                part = part.reshape(2, 2, *part.shape[1:])
                part = jnp.swapaxes(part, 0, 1)
            part, expo = halve(part, expo, mine_bit, send, FRONT - 1)
        scale = expo[None, :]
        part = (part * jnp.exp2(-scale)).astype(F16)
        for mine_bit, send in reversed(stages()):
            part = double(part, mine_bit, send)
        part = double(part, core, lambda a: flip(a, "mp", 0))
        part = part.astype(F32) * jnp.exp2(scale)
        pieces = jnp.swapaxes(part, 3, 4).reshape(2, 2, 2, hidden // 256, *part.shape[5:])
        table_out = []
        for part, top in table_parts:
            expo = exponent_of(top)
            part = part.reshape(2, 2, 2, 2, *part.shape[3:])
            for k, (mine_bit, send) in enumerate(stages()):
                if k == 2:
                    part = jnp.swapaxes(part, 0, 1)
                part, expo = halve(part, expo, mine_bit, send, PAD - 1)
            table_out.append(part)
        table_out = jnp.concatenate(table_out, axis=0)
    else:
        pieces = lax.psum(sums, ("dp", "mp")).reshape(2, 2, 2, *sums.shape[2:])
        table_out = jnp.concatenate([part for part, _ in table_parts], axis=3)
        table_out = table_out.transpose(0, 3, 1, 2, 4).reshape(2, fields * PAD, table_rows)
        upper = bit_of("mp", 1)
        away = lax.dynamic_index_in_dim(table_out, 1 - upper, 0, keepdims=False)
        table_out = lax.dynamic_index_in_dim(table_out, upper, 0, keepdims=False) + flip(away, "mp", 1)
        table_out = lax.psum_scatter(table_out, "dp", scatter_dimension=1, tiled=True)
    tables_grad = table_out.reshape(fields, PAD, -1)[:, :emb].reshape(cat, -1).T
    (cross_grad, deep_grad, small), over = assemble(pieces, rows, full, hidden)
    return (
        logit[0],
        small[6, 0],
        dense_grad,
        tables_grad,
        cross_grad,
        jnp.concatenate([small[0], over[full, 0 : full - hidden]]),
        deep_grad,
        small[1],
        jnp.concatenate([small[2], small[5, 0 : full - hidden]]),
        small[3],
        small[6, 1:2],
    )


def solution(mesh):
    placed = (
        P(None, "dp"),
        P(None, "dp"),
        P(None, ("dp", "mp")),
        P(None, ("dp", "mp")),
        P(("dp", "mp")),
        P("mp", None),
        P(),
        P(),
        P(),
        P(),
        P(),
        P(),
        P(),
    )
    return jax.shard_map(
        body,
        mesh=mesh,
        in_specs=placed,
        out_specs=(
            P(("dp", "mp")),
            P(),
            P(None, ("dp", "mp")),
            P(("mp", "dp"), None),
            P(),
            P(),
            P(),
            P(),
            P(),
            P(),
            P(),
        ),
        check_vma=False,
    )
```

time: 826 us -> 321 us (0.39); the launches traced: 812 us -> 318 us
  matrix products: 323 us -> 0 us
  waiting for transfers between devices: 253 us -> 63.5 us
  local copies, waits for them, and re-layouts: 157 us -> 41 us
  Pallas kernels: 0 us -> 115 us
  starting transfers between devices: 0.34 us -> 43.5 us
  blocking collectives: 41.2 us -> 0 us
  other arithmetic: 18.6 us -> 51.5 us
  between operations: 17.9 us -> 4.26 us
    dot_general x58 -> x0, matrix products: 323 us -> none  [the longest x26 168 us: lookup(): jnp.dot(onehot, piece[:, field * emb_width:(field + 1) * emb_width], pref...]
    reduce_scatter x2 -> x0, waiting for transfers between devices: 190 us -> none  [the longest x1 100 us: body(): lax.psum_scatter(lookup(part_ids, tables).astype(jnp.bfloat16), 'mp', sca...]
    concatenate x2 -> x0, local copies, waits for them, and re-layouts: 144 us -> none  [the longest x1 108 us: lookup(): return jnp.concatenate(blocks, axis=1)]
    pallas_call x0 -> x9, Pallas kernels: none -> 115 us  [the longest x4 31.4 us: lookup(): pl.pallas_call(lambda *refs: lookup_kernel(emb, blocks, *refs), out_shape...]
    ppermute x0 -> x35, waiting for transfers between devices: none -> 63.5 us  [the longest x19 30.4 us: flip(): return lax.ppermute(array, axis, [(i, i ^ 1 << bit) for i in range(size)])]
    all_gather x1 -> x0, waiting for transfers between devices: 61.6 us -> none  [body(): piece = lax.all_gather(demb_low, 'mp', axis=0, tiled=True)]
    ppermute x0 -> x35, starting transfers between devices: none -> 43.5 us  [the longest x19 14 us: flip(): return lax.ppermute(array, axis, [(i, i ^ 1 << bit) for i in range(size)])]
    psum x1 -> x0, blocking collectives: 41.2 us -> none  [body(): lax.psum((loss_sum, cross_weight_grad, cross_bias_grad, deep_weight_grad,...]
  transfers between devices with their start and end apart: 4 -> 35, of which waited for: 4 -> 16; matrix products, arithmetic and copies ran while one was open for 21% -> 16% of each run, Pallas kernels for 0% -> 17%
where the time goes in v1:
time: 321 us; the launch traced here: 318 us
  Pallas kernels  115 us (36%)
  waiting for transfers between devices  63.5 us (20%)
  other arithmetic  51.5 us (16%)
  starting transfers between devices  43.5 us (14%)
  local copies, waits for them, and re-layouts  41 us (13%)
  between operations  4.26 us (1%)
    pallas_call x4, Pallas kernels, lookup(): pl.pallas_call(lambda *refs: lookup_kernel(emb, blocks, *refs), out_shape...  31.4 us
    pallas_call x1, Pallas kernels, layers(): pl.pallas_call(lambda *refs: layers_kernel((fields, emb, dense, len(chunk...  31 us
    ppermute x19, waiting for transfers between devices, flip(): return lax.ppermute(array, axis, [(i, i ^ 1 << bit) for i in range(size)])  30.4 us
    ppermute x8, waiting for transfers between devices, crossed_flip(): lax.ppermute(array, ('dp', 'mp'), crossed_pairs(stage, lax.axis_size('dp'...  28.2 us
    pallas_call x2, Pallas kernels, spread(): pl.pallas_call(spread_kernel, grid=(count,), in_specs=[pl.BlockSpec((1, 2...  27.6 us
    pallas_call x1, Pallas kernels, weight_grads(): pl.pallas_call(lambda *refs: weight_kernel(rows, full, examples_all, *ref...  14.6 us
    ppermute x19, starting transfers between devices, flip(): return lax.ppermute(array, axis, [(i, i ^ 1 << bit) for i in range(size)])  14 us
    ppermute x4, starting transfers between devices, body(): got = lax.ppermute(part, ('dp', 'mp'), direct)  12.6 us
  transfers between devices with their start and end apart: 35, of which 16 were waited for; matrix products, arithmetic and copies ran while one was open for 16% of the time, Pallas kernels for 17%

profile of v1, /device:TPU:0, one launch (start us, length us, event | category | flops | bytes accessed | tf_op | source)
XLA Modules:
  0.0 318.4 jit_solution(3740935628700600421)
XLA Ops:
  0.6 2.8 fusion.59
  3.4 4.9 %collective-permute-start.1 = (bf16[312,1024]{1,0:T(8,128)(2,1)}, bf16[312,1024]{1,0:T(8,128)(2,1)}, u32[]{:S(2)}, u32[]{:S(2)}) collective-permute-start(bf16[312,1024]{1,0:T(8,128)(2,1)} %get-tuple-element.100.refs_2_), channel_id=1, source_target_pairs={{0,2},{2,0},{5,7},{7,5},{8,10},{10,8},{13,15},{15,13},{16,18},{18,... | collective-permute-start | bytes 1916936 | tf_op jit(solution)/shard_map/ppermute | solution.py:557
  8.4 1.9 collective-permute-start.5
  10.3 3.9 %collective-permute-start.9 = (bf16[312,1024]{1,0:T(8,128)(2,1)}, bf16[312,1024]{1,0:T(8,128)(2,1)}, u32[]{:S(2)}, u32[]{:S(2)}) collective-permute-start(bf16[312,1024]{1,0:T(8,128)(2,1)} %get-tuple-element.98.refs_2_), channel_id=1, source_target_pairs={{0,2},{2,0},{5,7},{7,5},{8,10},{10,8},{13,15},{15,13},{16,18},{18,... | collective-permute-start | bytes 1916936 | tf_op jit(solution)/shard_map/ppermute | solution.py:557
  15.2 1.9 collective-permute-start.13
  17.1 3.5 %fusion.57 = (bf16[1032,1032]{1,0:T(8,128)(2,1)}, bf16[1032,1032]{0,1:T(8,128)(2,1)S(1)}) fusion(bf16[1027,1027]{1,0:T(8,128)(2,1)} %param.19), kind=kLoop, calls=%fused_computation.200 | loop fusion | bytes 6369554 | tf_op jit(solution)/shard_map/jit(_pad)/pad | solution.py:573
  22.2 2.2 collective-permute-start.2
  25.1 2.1 collective-permute-start.6
  27.2 2.6 fusion.58
  31.0 3.3 %copy.24.refs_7_ = bf16[1032,1032]{1,0:T(8,128)(2,1)} copy(bf16[1032,1032]{0,1:T(8,128)(2,1)S(1)} %get-tuple-element.92) | data formatting | bytes 4260096 | tf_op jit(solution)/shard_map/transpose | solution.py:575
  34.3 4.1 %copy.25.refs_9_ = bf16[1024,1032]{1,0:T(8,128)(2,1)} copy(bf16[1024,1032]{0,1:T(8,128)(2,1)} %get-tuple-element.97) | data formatting | bytes 4227072 | tf_op jit(solution)/shard_map/transpose | solution.py:575
  39.8 2.6 collective-permute-start.14
  47.6 4.5 %collective-permute-done.10 = bf16[312,1024]{1,0:T(8,128)(2,1)S(1)} collective-permute-done((bf16[312,1024]{1,0:T(8,128)(2,1)}, bf16[312,1024]{1,0:T(8,128)(2,1)S(1)}, u32[]{:S(2)}, u32[]{:S(2)}) %collective-permute-start.10) | collective-permute-done | bytes 639008 | tf_op jit(solution)/shard_map/ppermute | solution.py:558
  55.8 9.2 %lookup.4.refs_0_ = f32[8,40,1536]{2,1,0:T(8,128)} custom-call(s32[8,1536]{1,0:T(8,128)} %get-tuple-element.133.refs_0_, s32[8,1536]{1,0:T(8,128)} %get-tuple-element.112.refs_1_, bf16[312,1024]{1,0:T(8,128)(2,1)} %get-tuple-element.100.refs_2_, bf16[312,1024]{1,0:T(8,128)(2,1)} %collective-permute-done.refs_3_, bf16[312,1024]{1,0:T(8,128)(2,1)} %copy-done.12, ...), custom_call_target="tpu_custom_call" | custom-call | flops 4026531840 | bytes 1966080 | tf_op jit(solution)/shard_map/lookup/pallas_call | solution.py:81
  65.2 9.0 %lookup.5.refs_1_ = f32[8,40,1536]{2,1,0:T(8,128)} custom-call(s32[8,1536]{1,0:T(8,128)} %get-tuple-element.39.refs_0_, s32[8,1536]{1,0:T(8,128)} %get-tuple-element.40.refs_1_, bf16[312,1024]{1,0:T(8,128)(2,1)} %get-tuple-element.99.refs_2_, bf16[312,1024]{1,0:T(8,128)(2,1)} %collective-permute-done.4.refs_3_, bf16[312,1024]{1,0:T(8,128)(2,1)} %copy-done.13, ...), custom_call_target="tpu_custom_call" | custom-call | flops 4026531840 | bytes 1966080 | tf_op jit(solution)/shard_map/lookup/pallas_call | solution.py:81
  75.1 9.0 %lookup.6.refs_2_ = f32[8,40,1536]{2,1,0:T(8,128)} custom-call(s32[8,1536]{1,0:T(8,128)} %get-tuple-element.42.refs_0_, s32[8,1536]{1,0:T(8,128)} %get-tuple-element.43.refs_1_, bf16[312,1024]{1,0:T(8,128)(2,1)} %get-tuple-element.98.refs_2_, bf16[312,1024]{1,0:T(8,128)(2,1)} %collective-permute-done.8.refs_3_, bf16[312,1024]{1,0:T(8,128)(2,1)} %copy-done.11, ...), custom_call_target="tpu_custom_call" | custom-call | flops 4026531840 | bytes 1966080 | tf_op jit(solution)/shard_map/lookup/pallas_call | solution.py:81
  85.5 4.2 %lookup.7.refs_3_ = f32[2,40,1536]{2,1,0:T(8,128)} custom-call(s32[2,1536]{1,0:T(2,128)} %slice.169.refs_0_, s32[2,1536]{1,0:T(2,128)} %slice.170.refs_1_, bf16[78,1024]{1,0:T(8,128)(2,1)} %copy-done.15, bf16[78,1024]{1,0:T(8,128)(2,1)} %copy-done.25, bf16[78,1024]{1,0:T(8,128)(2,1)} %copy-done.16, bf16[78,1024]{1,0:T(8,128)(2,1)} %copy-done.26), custom_call_target="tpu_custom_call" | custom-call | flops 1006632960 | bytes 491520 | tf_op jit(solution)/shard_map/lookup/pallas_call | solution.py:81
  94.4 31.0 %layers.1 = (f32[1,1536]{1,0:T(1,128)}, bf16[1040,1536]{1,0:T(8,128)(2,1)}, bf16[1040,1536]{1,0:T(8,128)(2,1)}, bf16[1024,1536]{1,0:T(8,128)(2,1)}, bf16[26,40,1...) custom-call(f32[8,40,1536]{2,1,0:T(8,128)} %lookup.4.refs_0_, ...), custom_call_target="tpu_custom_call" | custom-call | flops 13036290048 | bytes 41140224 | tf_op jit(solution)/shard_map/layers/pallas_call | solution.py:205
  125.4 14.6 %weight_grads.1 = (f32[2,4,4,528,128]{4,3,2,1,0:T(8,128)}, f32[8,128]{1,0:T(8,128)}) custom-call(bf16[1040,1536]{1,0:T(8,128)(2,1)} %get-tuple-element.48.refs_0_.refs_1_, bf16[1040,1536]{1,0:T(8,128)(2,1)} %get-tuple-element.48.refs_0_.refs_1_, bf16[1040,1536]{1,0:T(8,128)(2,1)} %get-tuple-element.49.refs_2_.refs_3_, ...), custom_call_target="tpu_custom_call" | custom-call | flops 6492782592 | bytes 21135360 | tf_op jit(solution)/shard_map/weight_grads/pallas_call | solution.py:297
  142.1 4.2 %fusion = f16[4,4,528,128]{3,2,1,0:T(8,128)(2,1)} fusion(f32[2,4,4,528,128]{4,3,2,1,0:T(8,128)} %get-tuple-element.54, s32[]{:T(128)S(6)} %select_n.287, f32[]{:T(128)S(6)} %sub.74, f32[]{:T(128)S(6)} %exp2.305, pred[528]{0:T(1024)(128)(4,1)S(1)} %iota_compare_fusion.1), kind=kLoop, calls=%fused_computation.2 | loop fusion | flops 3244032 | bytes 6488604 | tf_op jit(solution)/shard_map/convert_element_type | solution.py:421
  147.0 5.2 %compare_select_fusion.5 = (s32[26,2,1536]{2,1,0:T(2,128)}, s32[26,2,1536]{2,1,0:T(2,128)S(1)}) fusion(pred[]{:T(512)S(6)} %eq.100, s32[]{:T(128)S(6)} %and.104, s32[26,1,1536]{2,1,0:T(1,128)S(1)} %stack.70, s32[26,1,1536]{2,1,0:T(1,128)S(1)} %stack.69), kind=kLoop, calls=%fused_computation.40 | loop fusion | flops 6948864 | bytes 958469 | tf_op jit(solution)/shard_map/jit(_where)/select_n | solution.py:517
  152.3 2.7 bitcast_add_fusion
  155.0 2.0 copy-done.1
  159.1 3.0 fusion.18.hi_ref
  162.1 13.8 %spread.2 = (f32[2,4,2,520,128]{4,3,2,1,0:T(8,128)}, f32[8,128]{1,0:T(8,128)}) custom-call(s32[26,2,1536]{2,1,0:T(2,128)} %fusion.18.hi_ref, s32[26,2,1536]{2,1,0:T(2,128)} %get-tuple-element.77.lo_ref, bf16[26,40,1536]{2,1,0:T(8,128)(2,1)} %get-tuple-element.58.own_ref, bf16[26,40,1536]{2,1,0:T(8,128)(2,1)} %collective-permute-done.26.sib_ref), custom_call_target="tpu_custom_call" | custom-call | flops 6543114240 | bytes 17039360 | tf_op jit(solution)/shard_map/spread/pallas_call | solution.py:361
  178.9 2.2 bitcast_add_fusion.1
  182.9 13.7 %spread.3 = (f32[2,4,2,520,128]{4,3,2,1,0:T(8,128)}, f32[8,128]{1,0:T(8,128)}) custom-call(s32[26,2,1536]{2,1,0:T(2,128)} %fusion.18.hi_ref, s32[26,2,1536]{2,1,0:T(2,128)} %get-tuple-element.77.lo_ref, bf16[26,40,1536]{2,1,0:T(8,128)(2,1)} %get-tuple-element.58.own_ref, bf16[26,40,1536]{2,1,0:T(8,128)(2,1)} %collective-permute-done.26.sib_ref), custom_call_target="tpu_custom_call" | custom-call | flops 6543114240 | bytes 17039360 | tf_op jit(solution)/shard_map/spread/pallas_call | solution.py:361
  200.6 3.8 %fusion.4 = (f16[2,2,2,520,128]{4,3,2,1,0:T(8,128)(2,1)}, f16[2,2,2,520,128]{4,3,2,1,0:T(8,128)(2,1)S(1)}) fusion(f32[2,2,2,2,520,128]{5,4,3,2,1,0:T(8,128)} %bitcast.275, s32[]{:T(128)S(6)} %select_n.290, f32[]{:T(128)S(6)} %sub.75, f32[]{:T(128)S(6)} %exp2.329, pred[520]{0:T(1024)(128)(4,1)S(1)} %iota_compare_fusion, f32[]{:T(128)S(6)} %exp2.345, ...), kind=kLoop, calls=%fused_computation.15 | loop fusion | flops 3194880 | bytes 6390300 | tf_op jit(solution)/shard_map/convert_element_type | solution.py:421
  208.0 2.7 collective-permute-start.20
  211.7 4.3 %collective-permute-done.20 = f16[528,128]{1,0:T(8,128)(2,1)S(1)} collective-permute-done((f16[528,128]{1,0:T(8,128)(2,1)S(1)}, f16[528,128]{1,0:T(8,128)(2,1)S(1)}, u32[]{:S(2)}, u32[]{:S(2)}) %collective-permute-start.20) | collective-permute-done | bytes 135200 | tf_op jit(solution)/shard_map/ppermute | solution.py:386
  217.5 2.0 collective-permute-done.31
  221.3 9.6 %collective-permute-done.27 = f16[2,2,2,520,128]{4,3,2,1,0:T(8,128)(2,1)S(1)} collective-permute-done((f16[2,2,2,520,128]{4,3,2,1,0:T(8,128)(2,1)}, f16[2,2,2,520,128]{4,3,2,1,0:T(8,128)(2,1)S(1)}, u32[]{:S(2)}, u32[]{:S(2)}) %collective-permute-start.27) | collective-permute-done | bytes 1064992 | tf_op jit(solution)/shard_map/ppermute | solution.py:404
  230.9 1.9 bitcast_add_fusion.3
  237.5 3.5 %collective-permute-done.22 = f16[2,528,128]{2,1,0:T(8,128)(2,1)} collective-permute-done((f16[2,528,128]{2,1,0:T(8,128)(2,1)}, f16[2,528,128]{2,1,0:T(8,128)(2,1)}, u32[]{:S(2)}, u32[]{:S(2)}) %collective-permute-start.22) | collective-permute-done | bytes 270368 | tf_op jit(solution)/shard_map/ppermute | solution.py:386
  242.9 2.1 collective-permute-done.32
  245.0 5.7 %collective-permute-done.28 = f16[2,2,520,128]{3,2,1,0:T(8,128)(2,1)S(1)} collective-permute-done((f16[2,2,520,128]{3,2,1,0:T(8,128)(2,1)S(1)}, f16[2,2,520,128]{3,2,1,0:T(8,128)(2,1)S(1)}, u32[]{:S(2)}, u32[]{:S(2)}) %collective-permute-start.28) | collective-permute-done | bytes 532512 | tf_op jit(solution)/shard_map/ppermute | solution.py:404
  251.0 5.5 %collective-permute-done.23 = f16[2,2,528,128]{3,2,1,0:T(8,128)(2,1)S(1)} collective-permute-done((f16[2,2,528,128]{3,2,1,0:T(8,128)(2,1)S(1)}, f16[2,2,528,128]{3,2,1,0:T(8,128)(2,1)S(1)}, u32[]{:S(2)}, u32[]{:S(2)}) %collective-permute-start.23) | collective-permute-done | bytes 540704 | tf_op jit(solution)/shard_map/ppermute | solution.py:404
  260.3 5.8 %collective-permute-done.33 = f16[2,520,128]{2,1,0:T(8,128)(2,1)S(1)} collective-permute-done((f16[2,520,128]{2,1,0:T(8,128)(2,1)S(1)}, f16[2,520,128]{2,1,0:T(8,128)(2,1)S(1)}, u32[]{:S(2)}, u32[]{:S(2)}) %collective-permute-start.33) | collective-permute-done | bytes 266272 | tf_op jit(solution)/shard_map/ppermute | solution.py:386
  266.1 2.8 collective-permute-done.29
  269.0 3.4 %collective-permute-done.24 = f16[2,2,2,528,128]{4,3,2,1,0:T(8,128)(2,1)} collective-permute-done((f16[2,2,2,528,128]{4,3,2,1,0:T(8,128)(2,1)S(1)}, f16[2,2,2,528,128]{4,3,2,1,0:T(8,128)(2,1)}, u32[]{:S(2)}, u32[]{:S(2)}) %collective-permute-start.24) | collective-permute-done | bytes 1081376 | tf_op jit(solution)/shard_map/ppermute | solution.py:404
  272.4 1.9 select_bitcast_fusion.3
  274.3 1.9 pad_maximum_fusion
  277.2 2.6 collective-permute-start.30
  280.7 9.6 %collective-permute-done.30 = f16[520,128]{1,0:T(8,128)(2,1)S(1)} collective-permute-done((f16[520,128]{1,0:T(8,128)(2,1)}, f16[520,128]{1,0:T(8,128)(2,1)S(1)}, u32[]{:S(2)}, u32[]{:S(2)}) %collective-permute-start.30) | collective-permute-done | bytes 133152 | tf_op jit(solution)/shard_map/ppermute | solution.py:386
  290.3 2.5 collective-permute-done.34
  293.8 2.9 select_bitcast_fusion.1
  298.7 3.4 %copy-done = f32[2,2,2,2,2,528,128]{6,5,4,3,2,1,0:T(8,128)} copy-done((f32[2,2,2,2,2,528,128]{6,5,4,3,2,1,0:T(8,128)}, f32[2,2,2,2,2,528,128]{6,5,4,3,2,1,0:T(8,128)S(1)}, u32[]{:S(2)}) %copy-start) | copy-done | bytes 8650776
  303.5 10.1 %assemble.1 = (f32[1027,1027]{1,0:T(8,128)}, f32[1027,1024]{1,0:T(8,128)}, f32[8,1024]{1,0:T(8,128)}) custom-call(f32[2,2,2,4,528,128]{5,4,3,2,1,0:T(8,128)} %bitcast.270, f32[1032,128]{1,0:T(8,128)} %pad.29.refs_1_), custom_call_target="tpu_custom_call" | custom-call | bytes 16908288 | tf_op jit(solution)/shard_map/assemble/pallas_call | solution.py:477
  (191 shorter events, 62.0 us)
Async XLA Ops:
  3.4 18.8 %collective-permute-start.1 = (bf16[312,1024]{1,0:T(8,128)(2,1)}, bf16[312,1024]{1,0:T(8,128)(2,1)}, u32[]{:S(2)}, u32[]{:S(2)}) collective-permute-start(bf16[312,1024]{1,0:T(8,128)(2,1)} %get-tuple-element.100.refs_2_), channel_id=1, source_target_pairs={{0,2},{2,0},{5,7},{7,5},{8,10},{10,8},{13,15},{15,13},{16,18},{18,... | collective-permute-start | bytes 1916936 | tf_op jit(solution)/shard_map/ppermute | solution.py:557
  8.3 46.0 %collective-permute-start = (bf16[312,1024]{1,0:T(8,128)(2,1)}, bf16[312,1024]{1,0:T(8,128)(2,1)}, u32[]{:S(2)}, u32[]{:S(2)}) collective-permute-start(bf16[312,1024]{1,0:T(8,128)(2,1)} %get-tuple-element.100.refs_2_), channel_id=1, source_target_pairs={{0,1},{1,0},{2,3},{3,2},{4,5},{5,4},{6,7},{7,6},{8,9},{9,8},{10,11... | collective-permute-start | bytes 1916936 | tf_op jit(solution)/shard_map/ppermute | solution.py:386
  8.4 16.7 %collective-permute-start.5 = (bf16[312,1024]{1,0:T(8,128)(2,1)}, bf16[312,1024]{1,0:T(8,128)(2,1)}, u32[]{:S(2)}, u32[]{:S(2)}) collective-permute-start(bf16[312,1024]{1,0:T(8,128)(2,1)} %get-tuple-element.99.refs_2_), channel_id=1, source_target_pairs={{0,2},{2,0},{5,7},{7,5},{8,10},{10,8},{13,15},{15,13},{16,18},{18,... | collective-permute-start | bytes 1916936 | tf_op jit(solution)/shard_map/ppermute | solution.py:557
  10.3 29.5 %collective-permute-start.9 = (bf16[312,1024]{1,0:T(8,128)(2,1)}, bf16[312,1024]{1,0:T(8,128)(2,1)}, u32[]{:S(2)}, u32[]{:S(2)}) collective-permute-start(bf16[312,1024]{1,0:T(8,128)(2,1)} %get-tuple-element.98.refs_2_), channel_id=1, source_target_pairs={{0,2},{2,0},{5,7},{7,5},{8,10},{10,8},{13,15},{15,13},{16,18},{18,... | collective-permute-start | bytes 1916936 | tf_op jit(solution)/shard_map/ppermute | solution.py:557
  15.2 39.2 %copy-start.15 = (bf16[78,1024]{1,0:T(8,128)(2,1)}, bf16[78,1024]{1,0:T(8,128)(2,1)S(1)}, u32[]{:S(2)}) copy-start(bf16[78,1024]{1,0:T(8,128)(2,1)S(1)} %slice.172.refs_2_) | copy-start | bytes 479236
  15.2 24.5 %collective-permute-start.13 = (bf16[78,1024]{1,0:T(8,128)(2,1)S(1)}, bf16[78,1024]{1,0:T(8,128)(2,1)S(1)}, u32[]{:S(2)}, u32[]{:S(2)}) collective-permute-start(bf16[78,1024]{1,0:T(8,128)(2,1)S(1)} %slice.172.refs_2_), channel_id=1, source_target_pairs={{0,2},{2,0},{5,7},{7,5},{8,10},{10,8},{13,15},{15,13},{16,18},{18,... | collective-permute-start | bytes 479240 | tf_op jit(solution)/shard_map/ppermute | solution.py:557
  20.6 6.6 %copy-start.8 = (bf16[1027,1024]{1,0:T(8,128)(2,1)S(1)}, bf16[1027,1024]{1,0:T(8,128)(2,1)}, u32[]{:S(2)}) copy-start(bf16[1027,1024]{1,0:T(8,128)(2,1)} %param.21) | copy-start | bytes 6309892
  22.2 20.2 %collective-permute-start.2 = (bf16[312,1024]{1,0:T(8,128)(2,1)}, bf16[312,1024]{1,0:T(8,128)(2,1)}, u32[]{:S(2)}, u32[]{:S(2)}) collective-permute-start(bf16[312,1024]{1,0:T(8,128)(2,1)} %collective-permute-done.1), channel_id=1, source_target_pairs={{0,4},{2,6},{5,1},{7,3},{8,12},{10,14},{13,9},{15,11},{16,20},{18,... | collective-permute-start | bytes 1916936 | tf_op jit(solution)/shard_map/ppermute | solution.py:558
  25.1 21.3 %collective-permute-start.6 = (bf16[312,1024]{1,0:T(8,128)(2,1)}, bf16[312,1024]{1,0:T(8,128)(2,1)}, u32[]{:S(2)}, u32[]{:S(2)}) collective-permute-start(bf16[312,1024]{1,0:T(8,128)(2,1)} %collective-permute-done.5), channel_id=1, source_target_pairs={{0,4},{2,6},{5,1},{7,3},{8,12},{10,14},{13,9},{15,11},{16,20},{18,... | collective-permute-start | bytes 1916936 | tf_op jit(solution)/shard_map/ppermute | solution.py:558
  34.3 4.1 %copy-start.17 = (s32[1536]{0:T(1024)S(1)}, s32[1536]{0:T(1024)}, u32[]{:S(2)}) copy-start(s32[1536]{0:T(1024)} %param.17) | copy-start | bytes 18436
  39.7 25.3 %collective-permute-start.4 = (bf16[312,1024]{1,0:T(8,128)(2,1)}, bf16[312,1024]{1,0:T(8,128)(2,1)}, u32[]{:S(2)}, u32[]{:S(2)}) collective-permute-start(bf16[312,1024]{1,0:T(8,128)(2,1)} %get-tuple-element.99.refs_2_), channel_id=1, source_target_pairs={{0,1},{1,0},{2,3},{3,2},{4,5},{5,4},{6,7},{7,6},{8,9},{9,8},{10,11... | collective-permute-start | bytes 1916936 | tf_op jit(solution)/shard_map/ppermute | solution.py:386
  39.8 5.4 %collective-permute-start.14 = (bf16[78,1024]{1,0:T(8,128)(2,1)S(1)}, bf16[78,1024]{1,0:T(8,128)(2,1)S(1)}, u32[]{:S(2)}, u32[]{:S(2)}) collective-permute-start(bf16[78,1024]{1,0:T(8,128)(2,1)S(1)} %collective-permute-done.13), channel_id=1, source_target_pairs={{0,4},{2,6},{5,1},{7,3},{8,12},{10,14},{13,9},{15,11},{16,20},{18,... | collective-permute-start | bytes 479240 | tf_op jit(solution)/shard_map/ppermute | solution.py:558
  42.4 9.8 %collective-permute-start.10 = (bf16[312,1024]{1,0:T(8,128)(2,1)}, bf16[312,1024]{1,0:T(8,128)(2,1)S(1)}, u32[]{:S(2)}, u32[]{:S(2)}) collective-permute-start(bf16[312,1024]{1,0:T(8,128)(2,1)} %collective-permute-done.9), channel_id=1, source_target_pairs={{0,4},{2,6},{5,1},{7,3},{8,12},{10,14},{13,9},{15,11},{16,20},{18,... | collective-permute-start | bytes 1916936 | tf_op jit(solution)/shard_map/ppermute | solution.py:558
  44.9 9.4 %copy-start.12 = (bf16[312,1024]{1,0:T(8,128)(2,1)}, bf16[312,1024]{1,0:T(8,128)(2,1)S(1)}, u32[]{:S(2)}) copy-start(bf16[312,1024]{1,0:T(8,128)(2,1)S(1)} %broadcast_select_fusion.2.refs_4_) | copy-start | bytes 1916932
  45.2 9.3 %collective-permute-start.3 = (bf16[312,1024]{1,0:T(8,128)(2,1)S(1)}, bf16[312,1024]{1,0:T(8,128)(2,1)S(1)}, u32[]{:S(2)}, u32[]{:S(2)}) collective-permute-start(bf16[312,1024]{1,0:T(8,128)(2,1)S(1)} %broadcast_select_fusion.2.refs_4_), channel_id=1, source_target_pairs={{0,1},{1,0},{2,3},{3,2},{4,5},{5,4},{6,7},{7,6},{8,9},{9,8},{10,11... | collective-permute-start | bytes 1916936 | tf_op jit(solution)/shard_map/ppermute | solution.py:386
  46.3 18.6 %copy-start.16 = (bf16[78,1024]{1,0:T(8,128)(2,1)}, bf16[78,1024]{1,0:T(8,128)(2,1)S(1)}, u32[]{:S(2)}) copy-start(bf16[78,1024]{1,0:T(8,128)(2,1)S(1)} %broadcast_select_fusion.3.refs_4_) | copy-start | bytes 479236
  46.4 27.9 %collective-permute-start.8 = (bf16[312,1024]{1,0:T(8,128)(2,1)}, bf16[312,1024]{1,0:T(8,128)(2,1)}, u32[]{:S(2)}, u32[]{:S(2)}) collective-permute-start(bf16[312,1024]{1,0:T(8,128)(2,1)} %get-tuple-element.98.refs_2_), channel_id=1, source_target_pairs={{0,1},{1,0},{2,3},{3,2},{4,5},{5,4},{6,7},{7,6},{8,9},{9,8},{10,11... | collective-permute-start | bytes 1916936 | tf_op jit(solution)/shard_map/ppermute | solution.py:386
  47.6 17.4 %copy-start.13 = (bf16[312,1024]{1,0:T(8,128)(2,1)}, bf16[312,1024]{1,0:T(8,128)(2,1)S(1)}, u32[]{:S(2)}) copy-start(bf16[312,1024]{1,0:T(8,128)(2,1)S(1)} %broadcast_select_fusion.1.refs_4_) | copy-start | bytes 1916932
  52.1 13.1 %collective-permute-start.7 = (bf16[312,1024]{1,0:T(8,128)(2,1)S(1)}, bf16[312,1024]{1,0:T(8,128)(2,1)}, u32[]{:S(2)}, u32[]{:S(2)}) collective-permute-start(bf16[312,1024]{1,0:T(8,128)(2,1)S(1)} %broadcast_select_fusion.1.refs_4_), channel_id=1, source_target_pairs={{0,1},{1,0},{2,3},{3,2},{4,5},{5,4},{6,7},{7,6},{8,9},{9,8},{10,11... | collective-permute-start | bytes 1916936 | tf_op jit(solution)/shard_map/ppermute | solution.py:386
  54.3 10.6 %copy-start.11 = (bf16[312,1024]{1,0:T(8,128)(2,1)}, bf16[312,1024]{1,0:T(8,128)(2,1)S(1)}, u32[]{:S(2)}) copy-start(bf16[312,1024]{1,0:T(8,128)(2,1)S(1)} %broadcast_select_fusion.refs_4_) | copy-start | bytes 1916932
  54.4 29.8 %collective-permute-start.12 = (bf16[78,1024]{1,0:T(8,128)(2,1)S(1)}, bf16[78,1024]{1,0:T(8,128)(2,1)S(1)}, u32[]{:S(2)}, u32[]{:S(2)}) collective-permute-start(bf16[78,1024]{1,0:T(8,128)(2,1)S(1)} %slice.172.refs_2_), channel_id=1, source_target_pairs={{0,1},{1,0},{2,3},{3,2},{4,5},{5,4},{6,7},{7,6},{8,9},{9,8},{10,11... | collective-permute-start | bytes 479240 | tf_op jit(solution)/shard_map/ppermute | solution.py:386
  55.4 18.8 %collective-permute-start.11 = (bf16[312,1024]{1,0:T(8,128)(2,1)S(1)}, bf16[312,1024]{1,0:T(8,128)(2,1)S(1)}, u32[]{:S(2)}, u32[]{:S(2)}) collective-permute-start(bf16[312,1024]{1,0:T(8,128)(2,1)S(1)} %broadcast_select_fusion.refs_4_), channel_id=1, source_target_pairs={{0,1},{1,0},{2,3},{3,2},{4,5},{5,4},{6,7},{7,6},{8,9},{9,8},{10,11... | collective-permute-start | bytes 1916936 | tf_op jit(solution)/shard_map/ppermute | solution.py:386
  65.0 19.2 %collective-permute-start.15 = (bf16[78,1024]{1,0:T(8,128)(2,1)S(1)}, bf16[78,1024]{1,0:T(8,128)(2,1)S(1)}, u32[]{:S(2)}, u32[]{:S(2)}) collective-permute-start(bf16[78,1024]{1,0:T(8,128)(2,1)S(1)} %broadcast_select_fusion.3.refs_4_), channel_id=1, source_target_pairs={{0,1},{1,0},{2,3},{3,2},{4,5},{5,4},{6,7},{7,6},{8,9},{9,8},{10,11... | collective-permute-start | bytes 479240 | tf_op jit(solution)/shard_map/ppermute | solution.py:386
  84.1 7.6 %copy-start.21 = (f32[1024]{0:T(1024)S(1)}, f32[1024]{0:T(1024)}, u32[]{:S(2)}) copy-start(f32[1024]{0:T(1024)} %param.22) | copy-start | bytes 12292
  84.1 8.6 %copy-start.22 = (f32[1024]{0:T(1024)S(1)}, f32[1024]{0:T(1024)}, u32[]{:S(2)}) copy-start(f32[1024]{0:T(1024)} %param.24) | copy-start | bytes 12292
  146.3 6.0 %collective-permute-start.16 = (f16[4,4,528,128]{3,2,1,0:T(8,128)(2,1)}, f16[4,4,528,128]{3,2,1,0:T(8,128)(2,1)S(1)}, u32[]{:S(2)}, u32[]{:S(2)}) collective-permute-start(f16[4,4,528,128]{3,2,1,0:T(8,128)(2,1)} %fusion), channel_id=1, source_target_pairs={{0,1},{1,0},{2,3},{3,2},{4,5},{5,4},{6,7},{7,6},{8,9},{9,8},{10,11... | collective-permute-start | bytes 6488072 | tf_op jit(solution)/shard_map/ppermute | solution.py:386
  146.6 15.5 %collective-permute-start.26 = (bf16[26,40,1536]{2,1,0:T(8,128)(2,1)}, bf16[26,40,1536]{2,1,0:T(8,128)(2,1)}, u32[]{:S(2)}, u32[]{:S(2)}) collective-permute-start(bf16[26,40,1536]{2,1,0:T(8,128)(2,1)} %get-tuple-element.58.own_ref), channel_id=1, source_target_pairs={{0,1},{1,0},{2,3},{3,2},{4,5},{5,4},{6,7},{7,6},{8,9},{9,8},{10,11... | collective-permute-start | bytes 9584648 | tf_op jit(solution)/shard_map/ppermute | solution.py:386
  157.4 20.6 %collective-permute-start.17 = (f16[2,4,528,128]{3,2,1,0:T(8,128)(2,1)S(1)}, f16[2,4,528,128]{3,2,1,0:T(8,128)(2,1)S(1)}, u32[]{:S(2)}, u32[]{:S(2)}) collective-permute-start(f16[2,4,528,128]{3,2,1,0:T(8,128)(2,1)S(1)} %fusion.2), channel_id=1, source_target_pairs={{0,4},{1,3},{2,6},{3,1},{4,0},{5,7},{6,2},{7,5},{8,12},{9,11},{10,... | collective-permute-start | bytes 3244040 | tf_op jit(solution)/shard_map/ppermute | solution.py:404
  181.3 17.4 %collective-permute-start.18 = (f16[4,528,128]{2,1,0:T(8,128)(2,1)S(1)}, f16[4,528,128]{2,1,0:T(8,128)(2,1)S(1)}, u32[]{:S(2)}, u32[]{:S(2)}) collective-permute-start(f16[4,528,128]{2,1,0:T(8,128)(2,1)S(1)} %fusion.6), channel_id=1, source_target_pairs={{0,2},{1,5},{2,0},{3,7},{4,6},{5,1},{6,4},{7,3},{8,10},{9,13},{10,... | collective-permute-start | bytes 1622024 | tf_op jit(solution)/shard_map/ppermute | solution.py:404
  198.7 5.8 %copy-start.14 = (f16[4,528,128]{2,1,0:T(8,128)(2,1)}, f16[4,528,128]{2,1,0:T(8,128)(2,1)S(1)}, u32[]{:S(2)}) copy-start(f16[4,528,128]{2,1,0:T(8,128)(2,1)S(1)} %collective-permute-done.18) | copy-start | bytes 1622020
  199.0 8.0 %collective-permute-start.19 = (f16[2,528,128]{2,1,0:T(8,128)(2,1)S(1)}, f16[2,528,128]{2,1,0:T(8,128)(2,1)S(1)}, u32[]{:S(2)}, u32[]{:S(2)}) collective-permute-start(f16[2,528,128]{2,1,0:T(8,128)(2,1)S(1)} %fusion.12), channel_id=1, source_target_pairs={{0,8},{4,12},{8,0},{12,4},{16,24},{20,28},{24,16},{28,20},{1,9},{5... | collective-permute-start | bytes 811016 | tf_op jit(solution)/shard_map/ppermute | solution.py:386
  204.5 15.0 %collective-permute-start.31 = (f16[2,2,2,520,128]{4,3,2,1,0:T(8,128)(2,1)S(1)}, f16[2,2,2,520,128]{4,3,2,1,0:T(8,128)(2,1)S(1)}, u32[]{:S(2)}, u32[]{:S(2)}) collective-permute-start(f16[2,2,2,520,128]{4,3,2,1,0:T(8,128)(2,1)S(1)} %get-tuple-element.131), channel_id=1, source_target_pairs={{0,4},{1,3},{2,6},{3,1},{4,0},{5,7},{6,2},{7,5},{8,12},{9,11},{10,... | collective-permute-start | bytes 3194888 | tf_op jit(solution)/shard_map/ppermute | solution.py:404
  208.0 8.0 %collective-permute-start.20 = (f16[528,128]{1,0:T(8,128)(2,1)S(1)}, f16[528,128]{1,0:T(8,128)(2,1)S(1)}, u32[]{:S(2)}, u32[]{:S(2)}) collective-permute-start(f16[528,128]{1,0:T(8,128)(2,1)S(1)} %fusion.22), channel_id=1, source_target_pairs={{0,16},{4,20},{8,24},{12,28},{16,0},{20,4},{24,8},{28,12},{1,17},{... | collective-permute-start | bytes 405512 | tf_op jit(solution)/shard_map/ppermute | solution.py:386
  210.6 20.2 %collective-permute-start.27 = (f16[2,2,2,520,128]{4,3,2,1,0:T(8,128)(2,1)}, f16[2,2,2,520,128]{4,3,2,1,0:T(8,128)(2,1)S(1)}, u32[]{:S(2)}, u32[]{:S(2)}) collective-permute-start(f16[2,2,2,520,128]{4,3,2,1,0:T(8,128)(2,1)} %get-tuple-element.130), channel_id=1, source_target_pairs={{0,4},{1,3},{2,6},{3,1},{4,0},{5,7},{6,2},{7,5},{8,12},{9,11},{10,... | collective-permute-start | bytes 3194888 | tf_op jit(solution)/shard_map/ppermute | solution.py:404
  216.8 16.0 %collective-permute-start.21 = (f16[528,128]{1,0:T(8,128)(2,1)S(1)}, f16[528,128]{1,0:T(8,128)(2,1)S(1)}, u32[]{:S(2)}, u32[]{:S(2)}) collective-permute-start(f16[528,128]{1,0:T(8,128)(2,1)S(1)} %fusion.24), channel_id=1, source_target_pairs={{0,16},{4,20},{8,24},{12,28},{16,0},{20,4},{24,8},{28,12},{1,17},{... | collective-permute-start | bytes 405512 | tf_op jit(solution)/shard_map/ppermute | solution.py:386
  233.9 7.2 %collective-permute-start.22 = (f16[2,528,128]{2,1,0:T(8,128)(2,1)}, f16[2,528,128]{2,1,0:T(8,128)(2,1)}, u32[]{:S(2)}, u32[]{:S(2)}) collective-permute-start(f16[2,528,128]{2,1,0:T(8,128)(2,1)} %pad_maximum_fusion.4), channel_id=1, source_target_pairs={{0,8},{4,12},{8,0},{12,4},{16,24},{20,28},{24,16},{28,20},{1,9},{5... | collective-permute-start | bytes 811016 | tf_op jit(solution)/shard_map/ppermute | solution.py:386
  235.5 9.5 %collective-permute-start.32 = (f16[2,2,520,128]{3,2,1,0:T(8,128)(2,1)}, f16[2,2,520,128]{3,2,1,0:T(8,128)(2,1)S(1)}, u32[]{:S(2)}, u32[]{:S(2)}) collective-permute-start(f16[2,2,520,128]{3,2,1,0:T(8,128)(2,1)} %get-tuple-element.129), channel_id=1, source_target_pairs={{0,2},{1,5},{2,0},{3,7},{4,6},{5,1},{6,4},{7,3},{8,10},{9,13},{10,... | collective-permute-start | bytes 1597448 | tf_op jit(solution)/shard_map/ppermute | solution.py:404
  236.0 14.7 %collective-permute-start.28 = (f16[2,2,520,128]{3,2,1,0:T(8,128)(2,1)S(1)}, f16[2,2,520,128]{3,2,1,0:T(8,128)(2,1)S(1)}, u32[]{:S(2)}, u32[]{:S(2)}) collective-permute-start(f16[2,2,520,128]{3,2,1,0:T(8,128)(2,1)S(1)} %get-tuple-element.128), channel_id=1, source_target_pairs={{0,2},{1,5},{2,0},{3,7},{4,6},{5,1},{6,4},{7,3},{8,10},{9,13},{10,... | collective-permute-start | bytes 1597448 | tf_op jit(solution)/shard_map/ppermute | solution.py:404
  242.1 8.7 %copy-start.3 = (f32[2,2,2,520,128]{4,3,2,1,0:T(8,128)S(1)}, f32[2,2,2,520,128]{4,3,2,1,0:T(8,128)}, u32[]{:S(2)}) copy-start(f32[2,2,2,520,128]{4,3,2,1,0:T(8,128)} %copy-done.2) | copy-start | bytes 6389764
  242.3 14.1 %collective-permute-start.23 = (f16[2,2,528,128]{3,2,1,0:T(8,128)(2,1)S(1)}, f16[2,2,528,128]{3,2,1,0:T(8,128)(2,1)S(1)}, u32[]{:S(2)}, u32[]{:S(2)}) collective-permute-start(f16[2,2,528,128]{3,2,1,0:T(8,128)(2,1)S(1)} %pad_maximum_fusion.2), channel_id=1, source_target_pairs={{0,2},{1,5},{2,0},{3,7},{4,6},{5,1},{6,4},{7,3},{8,10},{9,13},{10,... | collective-permute-start | bytes 1622024 | tf_op jit(solution)/shard_map/ppermute | solution.py:404
  250.8 7.1 %copy-start.6 = (f32[2,2,520,128]{3,2,1,0:T(8,128)}, f32[2,2,520,128]{3,2,1,0:T(8,128)S(1)}, u32[]{:S(2)}) copy-start(f32[2,2,520,128]{3,2,1,0:T(8,128)S(1)} %bitcast_add_fusion.5) | copy-start | bytes 3194884
  251.0 7.0 %copy-start.4 = (f32[2,2,520,128]{3,2,1,0:T(8,128)}, f32[2,2,520,128]{3,2,1,0:T(8,128)S(1)}, u32[]{:S(2)}) copy-start(f32[2,2,520,128]{3,2,1,0:T(8,128)S(1)} %bitcast_add_fusion.6) | copy-start | bytes 3194884
  257.1 15.3 %collective-permute-start.24 = (f16[2,2,2,528,128]{4,3,2,1,0:T(8,128)(2,1)S(1)}, f16[2,2,2,528,128]{4,3,2,1,0:T(8,128)(2,1)}, u32[]{:S(2)}, u32[]{:S(2)}) collective-permute-start(f16[2,2,2,528,128]{4,3,2,1,0:T(8,128)(2,1)S(1)} %pad_maximum_fusion.1), channel_id=1, source_target_pairs={{0,4},{1,3},{2,6},{3,1},{4,0},{5,7},{6,2},{7,5},{8,12},{9,11},{10,... | collective-permute-start | bytes 3244040 | tf_op jit(solution)/shard_map/ppermute | solution.py:404
  258.2 7.9 %collective-permute-start.33 = (f16[2,520,128]{2,1,0:T(8,128)(2,1)S(1)}, f16[2,520,128]{2,1,0:T(8,128)(2,1)S(1)}, u32[]{:S(2)}, u32[]{:S(2)}) collective-permute-start(f16[2,520,128]{2,1,0:T(8,128)(2,1)S(1)} %get-tuple-element.127), channel_id=1, source_target_pairs={{0,8},{4,12},{8,0},{12,4},{16,24},{20,28},{24,16},{28,20},{1,9},{5... | collective-permute-start | bytes 798728 | tf_op jit(solution)/shard_map/ppermute | solution.py:386
  259.8 9.1 %collective-permute-start.29 = (f16[2,520,128]{2,1,0:T(8,128)(2,1)S(1)}, f16[2,520,128]{2,1,0:T(8,128)(2,1)S(1)}, u32[]{:S(2)}, u32[]{:S(2)}) collective-permute-start(f16[2,520,128]{2,1,0:T(8,128)(2,1)S(1)} %get-tuple-element.126), channel_id=1, source_target_pairs={{0,8},{4,12},{8,0},{12,4},{16,24},{20,28},{24,16},{28,20},{1,9},{5... | collective-permute-start | bytes 798728 | tf_op jit(solution)/shard_map/ppermute | solution.py:386
  276.2 17.6 %collective-permute-start.25 = (f16[2,2,2,2,528,128]{5,4,3,2,1,0:T(8,128)(2,1)}, f16[2,2,2,2,528,128]{5,4,3,2,1,0:T(8,128)(2,1)}, u32[]{:S(2)}, u32[]{:S(2)}) collective-permute-start(f16[2,2,2,2,528,128]{5,4,3,2,1,0:T(8,128)(2,1)} %pad_maximum_fusion), channel_id=1, source_target_pairs={{0,1},{1,0},{2,3},{3,2},{4,5},{5,4},{6,7},{7,6},{8,9},{9,8},{10,11... | collective-permute-start | bytes 6488072 | tf_op jit(solution)/shard_map/ppermute | solution.py:386
  277.2 13.2 %collective-permute-start.30 = (f16[520,128]{1,0:T(8,128)(2,1)}, f16[520,128]{1,0:T(8,128)(2,1)S(1)}, u32[]{:S(2)}, u32[]{:S(2)}) collective-permute-start(f16[520,128]{1,0:T(8,128)(2,1)} %get-tuple-element.124), channel_id=1, source_target_pairs={{0,16},{4,20},{8,24},{12,28},{16,0},{20,4},{24,8},{28,12},{1,17},{... | collective-permute-start | bytes 399368 | tf_op jit(solution)/shard_map/ppermute | solution.py:386
  280.4 12.4 %collective-permute-start.34 = (f16[520,128]{1,0:T(8,128)(2,1)S(1)}, f16[520,128]{1,0:T(8,128)(2,1)S(1)}, u32[]{:S(2)}, u32[]{:S(2)}) collective-permute-start(f16[520,128]{1,0:T(8,128)(2,1)S(1)} %get-tuple-element.125), channel_id=1, source_target_pairs={{0,16},{4,20},{8,24},{12,28},{16,0},{20,4},{24,8},{28,12},{1,17},{... | collective-permute-start | bytes 399368 | tf_op jit(solution)/shard_map/ppermute | solution.py:386
  (14 other events, 31.5 us)

commit v2 on v1

v2 whole, which is shorter than its diff:
```python
import math

import jax
import jax.numpy as jnp
from jax import lax
from jax.experimental import pallas as pl
from jax.experimental.pallas import tpu as pltpu
from jax.sharding import PartitionSpec as P

BF16, F32, F16 = jnp.bfloat16, jnp.float32, jnp.float16
HI = 256
SLOPE_TOP = 1.25
X_TOP = 6.0
FRONT = 8
PAD = 40
TILE = 256
WIDE = 512
GELU_S = math.sqrt(2.0 / math.pi)
GELU_C = 0.044715


def params(mebibytes):
    return pltpu.CompilerParams(vmem_limit_bytes=mebibytes * 1024 * 1024)


def cost(flops, moved):
    return pl.CostEstimate(flops=int(flops), bytes_accessed=int(moved), transcendentals=0)


def in_hbm(array):
    return pltpu.with_memory_space_constraint(array, pltpu.HBM)


def ceil_to(value, unit):
    return -(-value // unit) * unit


def dot_nn(left, right):
    return jnp.dot(left, right, preferred_element_type=F32)


def dot_nt(left, right, precision=None):
    return lax.dot_general(
        left, right, (((1,), (1,)), ((), ())), preferred_element_type=F32, precision=precision
    )


def onehot_rows(place, width):
    rows = lax.broadcasted_iota(jnp.int16, (HI, width), 0)
    return jnp.where(rows == place.astype(jnp.int16), jnp.ones((), BF16), jnp.zeros((), BF16))


def prepare_kernel(cw_ref, dw_ref, cb_ref, db_ref, hc_ref, hd_ref, ww_ref, wb_ref, cbo_ref, dbo_ref, hco_ref, hdo_ref, pad):
    full, hidden = dw_ref.shape
    rows = wb_ref.shape[0]
    pad[...] = jnp.zeros_like(pad)
    for source, base, width in ((dw_ref, 0, hidden), (cw_ref, hidden, full)):
        pad[0:full, 0:width] = source[...].astype(F32)
        if width < rows:
            pad[:, width:] = jnp.zeros((pad.shape[0], pad.shape[1] - width), F32)
        wide_width = hidden if base == 0 else rows
        wb_ref[:, base : base + wide_width] = pad[0:rows, 0:wide_width].astype(BF16)
        for r in range(0, wide_width, 128):
            n = min(128, wide_width - r)
            turned = pad[:, r : r + 128].T
            ww_ref[base + r : base + r + n, :] = turned[0:n, 0:rows].astype(BF16)
    for source, out, more in ((cb_ref, cbo_ref, 1.0), (db_ref, dbo_ref, 0.0), (hc_ref, hco_ref, 0.0), (hd_ref, hdo_ref, 0.0)):
        for r in range(0, out.shape[0], 128):
            n = min(128, out.shape[0] - r)
            line = source[:, r : r + 128]
            out[r : r + n, :] = (jnp.broadcast_to(line, (128, 128)).T + more)[0:n]


def prepare(cross_weight, deep_weight, cross_bias, deep_bias, head_cross, head_deep, rows):
    full, hidden = deep_weight.shape
    wide_rows = ceil_to(rows, 128)
    line = lambda v: jnp.pad(v, (0, ceil_to(v.shape[0], 128) - v.shape[0]))[None, :]
    shape = jax.ShapeDtypeStruct
    return pl.pallas_call(
        prepare_kernel,
        out_shape=[
            shape((hidden + rows, rows), BF16),
            shape((rows, hidden + rows), BF16),
            shape((rows, 128), F32),
            shape((hidden, 128), F32),
            shape((rows, 128), F32),
            shape((hidden, 128), F32),
        ],
        scratch_shapes=[pltpu.VMEM((wide_rows, wide_rows), F32)],
        compiler_params=params(16),
        cost_estimate=cost(0, 16 * rows * rows),
        name="prepare",
    )(cross_weight, deep_weight, line(cross_bias), line(deep_bias), line(head_cross), line(head_deep))


def lookup_kernel(emb, blocks, at_row, place_ref, block_ref, *refs):
    sources, out_ref, flat, packed = refs[0:4], refs[4], refs[5], refs[6]
    n_fields, examples = place_ref.shape
    rows = emb * n_fields
    for s, source in enumerate(sources):
        first = at_row if s < 2 else 0
        flat[s, 0:rows, :] = source[first : first + rows, :].astype(F32)
    for f in range(n_fields):
        for s in range(4):
            for b in range(blocks):
                piece = flat[s, emb * f : emb * f + PAD, b * HI : (b + 1) * HI]
                at = (s * blocks + b) * PAD
                packed[f, at : at + PAD, :] = piece.astype(BF16)

    def step(t, carry):
        at = pl.multiple_of(t * WIDE, WIDE)
        for f in range(n_fields):
            place = place_ref[f : f + 1, pl.ds(at, WIDE)]
            block = block_ref[f : f + 1, pl.ds(at, WIDE)]
            found = dot_nn(packed[f], onehot_rows(place, WIDE))
            acc = found[0:PAD]
            for b in range(1, 4 * blocks):
                acc = jnp.where(block == b, found[b * PAD : (b + 1) * PAD], acc)
            out_ref[f, :, pl.ds(at, WIDE)] = acc.astype(BF16)
        return carry

    lax.fori_loop(0, examples // WIDE, step, 0)


def lookup(place, block, sources, at_row, emb):
    n_fields, examples = place.shape
    width = sources[0].shape[1]
    blocks = width // HI
    n_rows = 4 * blocks * PAD
    return pl.pallas_call(
        lambda *refs: lookup_kernel(emb, blocks, at_row, *refs),
        out_shape=jax.ShapeDtypeStruct((n_fields, PAD, examples), BF16),
        scratch_shapes=[
            pltpu.VMEM((4, ceil_to(n_fields * emb, 8) + 8, width), F32),
            pltpu.VMEM((n_fields, n_rows, HI), BF16),
        ],
        compiler_params=params(16),
        cost_estimate=cost(2 * n_fields * n_rows * HI * examples, 4 * n_fields * PAD * examples),
        name="lookup",
    )(place, block, *sources)


def wide(column, width):
    return jnp.concatenate([column] * (width // 128), axis=1)


def fold(values):
    total = values[:, 0:128]
    for at in range(128, values.shape[1], 128):
        total = total + values[:, at : at + 128]
    return total


def peak(top, values):
    for r in range(0, values.shape[0], 8):
        top = jnp.maximum(top, jnp.abs(values[r : r + 8]))
    return top


def exponents(top):
    most = jnp.max(jnp.max(top, axis=1, keepdims=True), axis=0, keepdims=True)
    return jnp.broadcast_to(jnp.ceil(jnp.log(jnp.maximum(most, 1e-30)) * (1.0 / math.log(2.0))) - 14.0, (8, 128))


def layers_kernel(sizes, scale, *refs):
    fields, emb, dense, n_chunks, tiles = sizes
    chunks = refs[:n_chunks]
    (dv_ref, dm_ref, lab_ref, ww_ref, wb_ref, cb_ref, db_ref, hc_ref, hd_ref, hb_ref) = refs[n_chunks : n_chunks + 10]
    (logit_ref, xa_ref, grad_ref, demb_ref, dg_ref, hca_ref, hda_ref, sc_ref, expo_ref) = refs[
        n_chunks + 10 : n_chunks + 19
    ]
    top_ref, wws_ref, wbs_ref, sems, *scratch = refs[n_chunks + 19 :]
    loads = [
        pltpu.make_async_copy(ww_ref, wws_ref, sems.at[0]),
        pltpu.make_async_copy(wb_ref, wbs_ref, sems.at[1]),
    ]
    start = pl.program_id(0) == 0
    hidden = hda_ref.shape[0]
    rows = hca_ref.shape[0]
    width = TILE
    cat = fields * emb
    full = cat + dense
    step = 128
    cuts = [(a, min(a + step, rows)) for a in range(0, rows, step)]
    hid_cuts = [(a, min(a + step, hidden)) for a in range(0, hidden, step)]
    cols = [slice(k * TILE, (k + 1) * TILE) for k in range(tiles)]
    tall = xa_ref.shape[0]

    @pl.when(start)
    def _():
        for load in loads:
            load.start()
        hca_ref[...] = jnp.zeros_like(hca_ref)
        hda_ref[...] = jnp.zeros_like(hda_ref)
        sc_ref[...] = jnp.zeros_like(sc_ref)
        top_ref[...] = jnp.zeros_like(top_ref)

    def gather(k):
        x_ref = scratch[4 * k]
        f = 0
        for chunk in chunks:
            for c in range(chunk.shape[0]):
                x_ref[emb * f : emb * f + PAD, :] = chunk[c, :, cols[k]].astype(F32)
                f += 1
        x_ref[cat:full, :] = dv_ref[:, cols[k]] * dm_ref[:, cols[k]].astype(F32)
        x_ref[full:tall, :] = (
            lax.broadcasted_iota(jnp.int32, (tall - full, width), 0) == 0
        ).astype(F32)
        xa_ref[:, cols[k]] = x_ref[0:tall, :].astype(BF16)

    def forward(k):
        scratch[4 * k + 1][...] = dot_nn(wws_ref[...], xa_ref[0:rows, cols[k]])

    def logits(k):
        x_ref, pre_ref, act_ref, slope_ref = scratch[4 * k : 4 * k + 4]
        total = jnp.zeros((8, width), F32)
        for a, b in cuts:
            cp = pre_ref[hidden + a : hidden + b, :] + wide(cb_ref[a:b, :], width)
            pre_ref[hidden + a : hidden + b, :] = cp
            term = (x_ref[a:b, :] * cp) * wide(hc_ref[a:b, :], width)
            for r in range(0, b - a, 8):
                total = total + term[r : r + 8]
        for a, b in hid_cuts:
            v = pre_ref[a:b, :] + wide(db_ref[a:b, :], width)
            vv = v * v
            half = 0.5 + 0.5 * jnp.tanh(v * (GELU_S + (GELU_S * GELU_C) * vv))
            act = v * half
            act_ref[a:b, :] = act
            slope_ref[a:b, :] = half + (act * (1.0 - half)) * ((2.0 * GELU_S) + (6.0 * GELU_S * GELU_C) * vv)
            term = act * wide(hd_ref[a:b, :], width)
            for r in range(0, b - a, 8):
                total = total + term[r : r + 8]
        logit = jnp.sum(total, axis=0, keepdims=True) + hb_ref[0:1, 0:1]
        logit_ref[:, cols[k]] = logit
        labels = lab_ref[:, cols[k]].astype(F32)
        small = jnp.exp(-jnp.abs(logit))
        loss = jnp.maximum(logit, 0.0) + jnp.log1p(small) - labels * logit
        sig = jnp.where(logit >= 0.0, 1.0, small) / (1.0 + small)
        dlogit = (sig - labels) * scale
        sc_ref[0:1, :] += fold(loss)
        sc_ref[1:2, :] += fold(dlogit)
        top_ref[...] = jnp.maximum(top_ref[...], jnp.abs(dlogit))
        return dlogit

    def gradients(k, dlogit):
        x_ref, pre_ref, act_ref, slope_ref = scratch[4 * k : 4 * k + 4]
        for a, b in hid_cuts:
            hda_ref[a:b, :] += fold(dlogit * act_ref[a:b, :])
            dd = (dlogit * wide(hd_ref[a:b, :], width)) * slope_ref[a:b, :]
            grad_ref[a:b, cols[k]] = dd.astype(BF16)
        for a, b in cuts:
            cp = pre_ref[hidden + a : hidden + b, :]
            dx = dlogit * x_ref[a:b, :]
            hc = wide(hc_ref[a:b, :], width)
            hca_ref[a:b, :] += fold(dx * cp)
            dc = dx * hc
            if b == rows:
                dc = jnp.concatenate([dc, jnp.zeros((tall - rows, width), F32)], axis=0)
            grad_ref[hidden + a : hidden + a + dc.shape[0], cols[k]] = dc.astype(BF16)
            pre_ref[hidden + a : hidden + b, :] = (dlogit * hc) * cp

    def backward(k):
        x_ref, pre_ref = scratch[4 * k], scratch[4 * k + 1]
        x_ref[0:rows, :] = pre_ref[hidden:, :] + dot_nn(wbs_ref[...], grad_ref[0 : hidden + rows, cols[k]])

    def give(k):
        x_ref = scratch[4 * k]
        for f in range(fields):
            demb_ref[f, :, cols[k]] = x_ref[emb * f : emb * f + PAD, :].astype(BF16)
        dg_ref[:, cols[k]] = x_ref[cat:full, :] * dm_ref[:, cols[k]].astype(F32)

    dlogits = {}
    for phase, k in ORDER[tiles]:
        if phase == "w":
            pl.when(start)(loads[k].wait)
        elif phase == "x":
            gather(k)
        elif phase == "f":
            forward(k)
        elif phase == "l":
            dlogits[k] = logits(k)
        elif phase == "g":
            gradients(k, dlogits[k])
        elif phase == "b":
            backward(k)
        else:
            give(k)

    @pl.when(pl.program_id(0) == pl.num_programs(0) - 1)
    def _():
        each = jnp.zeros((8, 128), F32)
        for ref in (hca_ref, hda_ref, sc_ref):
            each = peak(each, ref[...])
        heads = jnp.zeros((8, 128), F32)
        for ref, most in ((hc_ref, X_TOP), (hd_ref, SLOPE_TOP)):
            heads = jnp.maximum(heads, most * peak(jnp.zeros((8, 128), F32), ref[...]))
        products = jnp.max(jnp.max(heads, axis=1, keepdims=True), axis=0, keepdims=True) * (
            X_TOP * tiles * TILE * pl.num_programs(0)
        )
        products = products * jnp.maximum(top_ref[:, 0:128], top_ref[:, 128:256])
        expo_ref[...] = exponents(jnp.maximum(each * 128.0, products))


ORDER = {
    2: [
        ("x", 0), ("x", 1), ("w", 0), ("f", 0), ("f", 1), ("l", 0), ("w", 1), ("l", 1),
        ("g", 0), ("b", 0), ("g", 1), ("b", 1), ("o", 0), ("o", 1),
    ],
}


TILES = 2


def layers(chunks, dense_values, dense_present, labels, weights, columns, emb, scale):
    fields = sum(c.shape[0] for c in chunks)
    dense, examples = dense_values.shape
    hidden = columns[1].shape[0]
    rows = columns[0].shape[0]
    tall = ceil_to(rows, 16)
    take = TILES * TILE
    column = lambda r: pl.BlockSpec((r, take), lambda t: (0, t))
    whole = lambda a: pl.BlockSpec(a.shape, lambda t: (0,) * a.ndim, pipeline_mode=pl.Buffered(1))
    kept = lambda r: pl.BlockSpec((r, 128), lambda t: (0, 0))
    shape = jax.ShapeDtypeStruct
    return pl.pallas_call(
        lambda *refs: layers_kernel((fields, emb, dense, len(chunks), TILES), scale, *refs),
        grid=(examples // take,),
        in_specs=[pl.BlockSpec((c.shape[0], PAD, take), lambda t: (0, 0, t)) for c in chunks]
        + [column(dense), column(dense), column(1)]
        + [pl.BlockSpec(memory_space=pltpu.HBM) for _ in weights]
        + [whole(a) for a in columns],
        out_specs=[
            column(1),
            column(tall),
            column(hidden + tall),
            pl.BlockSpec((fields, PAD, take), lambda t: (0, 0, t)),
            column(dense),
            kept(rows),
            kept(hidden),
            kept(8),
            kept(8),
        ],
        out_shape=[
            shape((1, examples), F32),
            shape((tall, examples), BF16),
            shape((hidden + tall, examples), BF16),
            shape((fields, PAD, examples), BF16),
            shape((dense, examples), F32),
            shape((rows, 128), F32),
            shape((hidden, 128), F32),
            shape((8, 128), F32),
            shape((8, 128), F32),
        ],
        scratch_shapes=[pltpu.VMEM((8, TILE), F32)]
        + [pltpu.VMEM(w.shape, BF16) for w in weights]
        + [pltpu.SemaphoreType.DMA((2,))]
        + [
            pltpu.VMEM((tall, TILE), F32),
            pltpu.VMEM((rows + hidden, TILE), F32),
            pltpu.VMEM((hidden, TILE), F32),
            pltpu.VMEM((hidden, TILE), F32),
        ]
        * TILES,
        compiler_params=params(40),
        cost_estimate=cost(2 * examples * rows * (2 * rows + 2 * hidden), 9 * 2**20 + 20 * rows * examples),
        name="layers",
    )(*chunks, dense_values, dense_present, labels, *map(in_hbm, weights), *columns)


def weight_kernel(rows, examples_all, half_ref, *refs):
    xa_ref, dd_ref, dc_ref, dct_ref, hc_ref, hct_ref, hd_ref, sc_ref, expo_ref, out_ref, over = refs
    quarter = out_ref.shape[2] - FRONT
    half, j = half_ref[0], pl.program_id(0)
    first = half * pl.num_programs(0) + j == 0
    x = xa_ref[0:rows, :]
    hidden = over.shape[1] - 128

    @pl.when(j == 0)
    def _():
        tail = dot_nt(x, dct_ref[...])
        tail = jnp.concatenate([tail, jnp.zeros((rows, 128 - 16), F32)], axis=1)
        for r in range(0, hidden, 128):
            over[:, r : r + 128] = tail[r : r + 128].T[0:8]
        last = jnp.concatenate([tail[hidden:rows], jnp.zeros((128 - rows + hidden, 128), F32)], axis=0)
        over[:, hidden:] = last.T[0:8]

    deep = dot_nt(x, dd_ref[...])
    cross = dot_nt(x, dc_ref[...])
    at = pl.multiple_of((half * pl.num_programs(0) + j) * TILE, TILE)
    total = lambda ref: jnp.sum(ref[...].T, axis=0, keepdims=True)
    row = lax.broadcasted_iota(jnp.int32, (8, TILE), 0)
    heads = jnp.where(row == 0, total(hc_ref), jnp.where(row == 1, total(hd_ref), 0.0))
    zeros = lambda n, m: jnp.zeros((n, m), F32)
    corner = jnp.concatenate([over[0:3, hidden:], zeros(3, TILE - 128)], axis=1)
    small = jnp.concatenate([zeros(2, TILE), corner, zeros(3, TILE)], axis=0)
    ends = jnp.concatenate([hct_ref[...], zeros(120, 128)], axis=0)
    ends = jnp.concatenate([total(ends), zeros(1, TILE - 128)], axis=1)
    sums = jnp.sum(sc_ref[...], axis=1, keepdims=True)
    lane = lax.broadcasted_iota(jnp.int32, (8, TILE), 1)
    scalars = jnp.where(lane == 0, sums[0:1] / examples_all, jnp.where(lane == 1, sums[1:2], 0.0))
    small = small + jnp.where(row == 5, ends, 0.0) + jnp.where(row == 6, scalars, 0.0)
    heads = heads + jnp.where(first, small, 0.0)
    parts = [(0, deep), (rows, cross), (2 * rows, over[:, pl.ds(at, TILE)]), (2 * rows + 8, heads)]
    for q in range(4):
        for h in range(2):
            out_ref[q, h, 0:FRONT, :] = expo_ref[...]
    for base, part in parts:
        at = 0
        while at < part.shape[0]:
            q, r = divmod(base + at, quarter)
            n = min(part.shape[0] - at, quarter - r)
            place = jnp.where(half == 0, (0, 2, 1, 3)[q], q)
            for h in range(2):
                out_ref[place, h, FRONT + r : FRONT + r + n, :] = part[at : at + n, h * 128 : (h + 1) * 128]
            at += n


def weight_grads(half, xa, grads, hca, hda, sc, expo, examples_all):
    tall, examples = xa.shape
    rows, hidden = hca.shape[0], hda.shape[0]
    quarter = ceil_to(2 * rows + 16, 32) // 4
    steps = hidden // TILE // 2
    return pl.pallas_call(
        lambda *refs: weight_kernel(rows, examples_all, *refs),
        grid_spec=pltpu.PrefetchScalarGridSpec(
            num_scalar_prefetch=1,
            grid=(steps,),
            in_specs=[
                pl.BlockSpec((tall, examples), lambda j, h: (0, 0), pipeline_mode=pl.Buffered(1)),
                pl.BlockSpec((TILE, examples), lambda j, h: (h[0] * steps + j, 0)),
                pl.BlockSpec((TILE, examples), lambda j, h: (2 * steps + h[0] * steps + j, 0)),
                pl.BlockSpec((16, examples), lambda j, h: (2 * hidden // 16, 0)),
                pl.BlockSpec((TILE, 128), lambda j, h: (h[0] * steps + j, 0)),
                pl.BlockSpec((8, 128), lambda j, h: (hidden // 8, 0)),
                pl.BlockSpec((TILE, 128), lambda j, h: (h[0] * steps + j, 0)),
                pl.BlockSpec((8, 128), lambda j, h: (0, 0)),
                pl.BlockSpec((8, 128), lambda j, h: (0, 0)),
            ],
            out_specs=pl.BlockSpec((4, 2, FRONT + quarter, 128), lambda j, h: (0, j, 0, 0)),
            scratch_shapes=[pltpu.VMEM((8, hidden + 128), F32)],
        ),
        out_shape=jax.ShapeDtypeStruct((4, 2 * steps, FRONT + quarter, 128), F32),
        compiler_params=params(16),
        cost_estimate=cost(2 * examples * rows * hidden, 10 * rows * hidden),
        name="weight_grads",
    )(half.reshape(1).astype(jnp.int32), xa, *[in_hbm(grads)] * 3, *map(in_hbm, (hca, hca, hda)), sc, expo)


def spread_kernel(first, core_ref, place_ref, block_ref, own_ref, sib_ref, out_ref, expo_ref, top_ref):
    count, _, examples = own_ref.shape
    n_blocks = out_ref.shape[0] * out_ref.shape[1]

    @pl.when(pl.program_id(0) == 0)
    def _():
        top_ref[...] = jnp.zeros_like(top_ref)

    core = core_ref[0]
    every = []
    for k in range(count):
        f = first + pl.program_id(0) * count + k
        sums = jnp.zeros((n_blocks * PAD, HI), F32)
        for s, ref in enumerate((own_ref, sib_ref)):
            base = (core if s == 0 else 1 - core) * examples
            for at in range(0, examples, WIDE):
                cols = pl.ds(pl.multiple_of(base + at, WIDE), WIDE)
                place = place_ref[pl.ds(f, 1), cols]
                block = block_ref[pl.ds(f, 1), cols]
                grads = ref[k, :, at : at + WIDE].astype(F32)
                chosen = [jnp.where(block == b, grads, 0.0) for b in range(n_blocks)]
                chosen = jnp.concatenate(chosen, axis=0).astype(BF16)
                sums = sums + dot_nt(chosen, onehot_rows(place, WIDE))
        every.append(sums)
    for k, sums in enumerate(every):
        top_ref[...] = peak(top_ref[...], sums)
        for b in range(n_blocks):
            for h in range(2):
                out_ref[b // out_ref.shape[1], b % out_ref.shape[1], h, k * PAD : (k + 1) * PAD] = sums[
                    b * PAD : (b + 1) * PAD, h * 128 : (h + 1) * 128
                ]

    @pl.when(pl.program_id(0) == pl.num_programs(0) - 1)
    def _():
        expo_ref[...] = exponents(jnp.maximum(top_ref[:, 0:128], top_ref[:, 128:256]))


def spread(core, place, block, own, sib, first, count, blocks):
    fields, _, examples = own.shape
    whole = lambda a: pl.BlockSpec(a.shape, lambda f: (0, 0), pipeline_mode=pl.Buffered(1))
    take = 2
    return pl.pallas_call(
        lambda *refs: spread_kernel(first, *refs),
        grid=(count // take,),
        in_specs=[pl.BlockSpec(memory_space=pltpu.SMEM), whole(place), whole(block)]
        + [pl.BlockSpec((take, PAD, examples), lambda f: (f + first // take, 0, 0))] * 2,
        out_specs=[
            pl.BlockSpec((2, blocks, 2, take * PAD, 128), lambda f: (0, 0, 0, f, 0)),
            pl.BlockSpec((8, 128), lambda f: (0, 0)),
        ],
        out_shape=[
            jax.ShapeDtypeStruct((2, blocks, 2, count * PAD, 128), F32),
            jax.ShapeDtypeStruct((8, 128), F32),
        ],
        scratch_shapes=[pltpu.VMEM((8, HI), F32)],
        compiler_params=params(10),
        cost_estimate=cost(8 * count * blocks * PAD * HI * examples, 4 * count * PAD * 16 * 128 * blocks),
        name="spread",
    )(core.reshape(1).astype(jnp.int32), place, block, own, sib)


def flip(array, axis, bit):
    size = lax.axis_size(axis)
    return lax.ppermute(array, axis, [(i, i ^ (1 << bit)) for i in range(size)])


def bit_of(axis, bit):
    return (lax.axis_index(axis) >> bit) & 1


def crossed_pairs(stage, n_dp, n_mp):
    pairs = []
    for d in range(n_dp):
        for m in range(n_mp):
            along_dp = (m & 1) == stage
            to = (d ^ 1, m) if along_dp else (d, m ^ 2)
            pairs.append((d * n_mp + m, to[0] * n_mp + to[1]))
    return pairs


def crossed_flip(array, stage):
    return lax.ppermute(array, ("dp", "mp"), crossed_pairs(stage, lax.axis_size("dp"), lax.axis_size("mp")))


def crossed_bit(stage):
    return jnp.where(bit_of("mp", 0) == stage, bit_of("dp", 0), bit_of("mp", 1))


def after(value, token):
    return lax.optimization_barrier((value, token))[0]


def encode(values, expo, at):
    row = lax.broadcasted_iota(jnp.int32, values.shape, values.ndim - 2)
    here = expo.reshape((1,) * (values.ndim - 1) + (128,))
    return jnp.where(row == at, here, values * jnp.exp2(-here)).astype(F16)


def add(kept, expo, got, at):
    theirs = got[(0,) * (got.ndim - 2) + (at,)].astype(F32)
    total = kept + got.astype(F32) * jnp.exp2(theirs).reshape((1,) * (got.ndim - 1) + (128,))
    return total, jnp.maximum(expo, theirs) + 1.0


def reduction(acc, expo, at, z_dim):
    for k, (mine, send) in enumerate(stages()):
        if k == 2:
            acc = jnp.swapaxes(acc.reshape(2, 2, *acc.shape[z_dim:]), 0, 1)
        away = lax.dynamic_index_in_dim(acc, 1 - mine, 0, keepdims=False)
        kept = lax.dynamic_index_in_dim(acc, mine, 0, keepdims=False)
        message = encode(away, expo, at)
        got = send(message)
        token = yield message
        acc, expo = add(kept, expo, after(got, token), at)
    yield acc, expo


def gathering(piece, core):
    for mine, send in [*reversed(stages()), (core, lambda a: flip(a, "mp", 0))]:
        other = send(piece)
        token = yield piece
        other = after(other, token)
        low = mine == 0
        piece = jnp.stack([jnp.where(low, piece, other), jnp.where(low, other, piece)], axis=0)
    yield piece


def stages():
    return [
        (crossed_bit(0), lambda a: crossed_flip(a, 0)),
        (crossed_bit(1), lambda a: crossed_flip(a, 1)),
        (bit_of("dp", 1), lambda a: flip(a, "dp", 1)),
        (bit_of("dp", 2), lambda a: flip(a, "dp", 2)),
    ]


def assemble_kernel(rows, full, in_ref, over_ref, cross_ref, deep_ref, vec_ref):
    t = pl.program_id(0)
    last = pl.num_programs(0) - 1

    @pl.when(t < last)
    def _():
        for h in range(2):
            cols = slice(h * 128, (h + 1) * 128)
            parts = []
            for q in range(4):
                ahead = jnp.where(t < last // 2, q % 2, q // 2)
                parts.append(in_ref[0, ahead, q // 2 + q % 2 - ahead, h, 0, FRONT:, :])
            every = jnp.concatenate(parts, axis=0)
            deep_ref[:, cols] = every[0:full]
            cross_ref[:, cols] = every[rows : rows + full]
            vec_ref[0:1, cols] = every[rows + full : rows + full + 1]
            vec_ref[1:2, cols] = every[full : full + 1]
            vec_ref[2:4, cols] = every[2 * rows + 8 : 2 * rows + 10]
            vec_ref[4:8, cols] = every[2 * rows + 12 : 2 * rows + 16]

    @pl.when(t == last)
    def _():
        cross_ref[:, 0:128] = over_ref[0:full, :]


def assemble(pieces, rows, full, hidden):
    steps = hidden // 256
    quarter = pieces.shape[5] - FRONT
    half = steps // 2
    spare = pieces[:, 1, 1, :, :, FRONT + quarter - 16 :, :].transpose(3, 0, 2, 1, 4).reshape(16, hidden)
    extra = full - hidden
    over = jnp.concatenate([spare[0:extra], spare[10 : 10 + extra, 0 : rows - hidden]], axis=1)
    over = jnp.pad(over.T, ((0, 0), (0, 128 - extra)))
    now = lambda t: jnp.minimum(t, steps - 1)
    return pl.pallas_call(
        lambda *refs: assemble_kernel(rows, full, *refs),
        grid=(steps + 1,),
        in_specs=[
            pl.BlockSpec(
                (1, 2, 2, 2, 1, FRONT + quarter, 128), lambda t: (now(t) // half, 0, 0, 0, now(t) % half, 0, 0)
            ),
            pl.BlockSpec((rows, 128), lambda t: (0, 0)),
        ],
        out_specs=[
            pl.BlockSpec((full, 256), lambda t: (0, t)),
            pl.BlockSpec((full, 256), lambda t: (0, now(t))),
            pl.BlockSpec((8, 256), lambda t: (0, now(t))),
        ],
        out_shape=[
            jax.ShapeDtypeStruct((full, full), F32),
            jax.ShapeDtypeStruct((full, hidden), F32),
            jax.ShapeDtypeStruct((8, hidden), F32),
        ],
        compiler_params=params(10),
        cost_estimate=cost(0, 16 * rows * hidden),
        name="assemble",
    )(pieces, over), over


def table_place(ids, table_rows, n_dp, core):
    upper = ids // (2 * table_rows)
    rest = ids % table_rows
    if n_dp == 8:
        piece = table_rows // n_dp
        at = rest // piece
        low = at % 2
        first = jnp.where(core == 0, low, upper)
        second = jnp.where(core == 0, upper, low)
        block = first * 4 + second * 2 + at // 4
        place = (at // 2) % 2 * piece + rest % piece
    else:
        block = upper * (table_rows // HI) + rest // HI
        place = rest % HI
    return place, jnp.where((ids // table_rows) % 2 == core, block, -1)


def body(
    field_ids,
    field_present,
    dense_values,
    dense_present,
    clicked,
    tables,
    cross_weight,
    cross_bias,
    deep_weight,
    deep_bias,
    head_cross,
    head_deep,
    head_bias,
):
    fields, batch_group = field_ids.shape
    table_rows, cat = tables.shape
    emb = cat // fields
    full, hidden = deep_weight.shape
    dense = full - cat
    n_dp, n_mp = lax.axis_size("dp"), lax.axis_size("mp")
    examples = batch_group // n_mp
    examples_all = batch_group * n_dp
    blocks = table_rows // HI
    rows = ceil_to(full + 1, 8)
    me = lax.axis_index("mp")
    core = me & 1

    chosen = jnp.where(field_present > 0, field_ids, 0)
    own_ids = lax.dynamic_slice_in_dim(chosen, me * examples, examples, 1)
    place_own = own_ids & (HI - 1)
    block_own = (own_ids // HI) ^ (me * blocks)
    pair_ids = lax.dynamic_slice_in_dim(chosen, (me - core) * examples, 2 * examples, 1)
    place, block = table_place(pair_ids, table_rows, n_dp, core)

    columns = tables.T
    cuts = [(0, 11), (11, 22), (22, fields)]
    far = [flip(columns[a * emb : b * emb], "mp", 1) for a, b in cuts]
    near = flip(columns, "mp", 0)
    weights = prepare(cross_weight, deep_weight, cross_bias, deep_bias, head_cross, head_deep, rows)
    token = weights[0]
    found = []
    for k, (a, b) in enumerate(cuts):
        far_near = flip(after(far[k], token), "mp", 0)
        found.append(lookup(place_own[a:b], block_own[a:b], (columns, near, far[k], far_near), a * emb, emb))
        token = found[-1]

    logit, xa, grads, demb, dense_grad, hca, hda, sc, expo = layers(
        found,
        dense_values,
        dense_present,
        clicked[None, :],
        weights[:2],
        (*weights[2:], jnp.broadcast_to(head_bias[:, None], (8, 128))),
        emb,
        1.0 / math.sqrt(examples_all),
    )
    demb_sib = flip(demb, "mp", 0)
    grad_args = (xa, grads, hca, hda, sc, expo, examples_all)
    away = weight_grads(1 - core, *grad_args)
    if n_dp == 8:
        away = encode(away, expo[0], FRONT - 1)
    got = flip(away, "mp", 0)
    sums = weight_grads(after(core, away), *grad_args)
    halves = [(0, 12), (12, fields)]

    def table_part(token, k):
        a, b = halves[k]
        part, top = spread(core, place, block, after(demb, token), demb_sib, a, b - a, blocks)
        return part, top[0]

    if n_dp == 8:
        got = after(got, sums)
        both, expo = add(sums, expo[0], got, FRONT - 1)
        both = both.reshape(2, 2, *sums.shape[1:])
        weight_chain = reduction(both, expo, FRONT - 1, 1)
        token = next(weight_chain)
        table_chains = []
        for k in range(2):
            part, top = table_part(token, k)
            part = part.reshape(2, 2, 2, 2, *part.shape[3:])
            table_chains.append(reduction(part, top, PAD - 1, 2))
            token = next(table_chains[k])
            token = weight_chain.send(token)
        token = table_chains[0].send(token)
        token = weight_chain.send(token)
        token = table_chains[1].send(token)
        token = table_chains[0].send(token)
        total, expo = weight_chain.send(token)
        total = (total * jnp.exp2(-expo)[None, :]).astype(F16)
        weight_chain = gathering(total, core)
        token = next(weight_chain)
        token = table_chains[1].send(token)
        token = table_chains[0].send(token)
        token = weight_chain.send(token)
        token = table_chains[1].send(token)
        token = weight_chain.send(token)
        first_part, _ = table_chains[0].send(token)
        token = weight_chain.send(first_part)
        second_part, _ = table_chains[1].send(token)
        token = weight_chain.send(second_part)
        pieces = weight_chain.send(token)
        pieces = pieces.astype(F32) * jnp.exp2(expo)
        table_out = jnp.concatenate([first_part, second_part], axis=0)
    else:
        summed = lax.psum(sums + got, "dp")
        summed = summed + flip(summed, "mp", 1)
        pieces = lax.all_gather(summed, "mp")[0:2].reshape(2, 2, 2, 2, 2, *sums.shape[2:])
        pieces = jnp.swapaxes(pieces, 3, 4)
        table_out = jnp.concatenate([table_part(sums, k)[0] for k in range(2)], axis=3)
        table_out = table_out.transpose(0, 3, 1, 2, 4).reshape(2, fields * PAD, table_rows)
        upper = bit_of("mp", 1)
        away = lax.dynamic_index_in_dim(table_out, 1 - upper, 0, keepdims=False)
        table_out = lax.dynamic_index_in_dim(table_out, upper, 0, keepdims=False) + flip(away, "mp", 1)
        table_out = lax.psum_scatter(table_out, "dp", scatter_dimension=1, tiled=True)
    tables_grad = table_out.reshape(fields, PAD, -1)[:, :emb].reshape(cat, -1).T
    (cross_grad, deep_grad, small), over = assemble(pieces, rows, full, hidden)
    return (
        logit[0],
        small[6, 0],
        dense_grad,
        tables_grad,
        cross_grad,
        jnp.concatenate([small[0], over[full, 0 : full - hidden]]),
        deep_grad,
        small[1],
        jnp.concatenate([small[2], small[5, 0 : full - hidden]]),
        small[3],
        small[6, 1:2],
    )


def solution(mesh):
    placed = (
        P(None, "dp"),
        P(None, "dp"),
        P(None, ("dp", "mp")),
        P(None, ("dp", "mp")),
        P(("dp", "mp")),
        P("mp", None),
        P(),
        P(),
        P(),
        P(),
        P(),
        P(),
        P(),
    )
    return jax.shard_map(
        body,
        mesh=mesh,
        in_specs=placed,
        out_specs=(
            P(("dp", "mp")),
            P(),
            P(None, ("dp", "mp")),
            P(("mp", "dp"), None),
            P(),
            P(),
            P(),
            P(),
            P(),
            P(),
            P(),
        ),
        check_vma=False,
    )
```

time: 321 us -> 264 us (0.82)
  other arithmetic: 51.5 us -> 30.2 us
  local copies, waits for them, and re-layouts: 41 us -> 24.2 us
  starting transfers between devices: 43.5 us -> 31.5 us
  Pallas kernels: 115 us -> 104 us
  waiting for transfers between devices: 63.5 us -> 68.3 us
    ppermute x8 -> x0, starting transfers between devices: 20.9 us -> none  [the longest x4 12.6 us: body(): got = lax.ppermute(part, ('dp', 'mp'), direct)]
    unnamed x54 -> x68, local copies, waits for them, and re-layouts: 9.63 us -> 18.7 us
    ppermute x19 -> x18, waiting for transfers between devices: 30.4 us -> 39.5 us  [flip(): return lax.ppermute(array, axis, [(i, i ^ 1 << bit) for i in range(size)])]
    pallas_call x8 -> x9, Pallas kernels: 83.8 us -> 75.1 us  [the longest x2 25.1 us: weight_grads(): pl.pallas_call(lambda *refs: weight_kernel(rows, examples_all, *refs), gr...]
    transpose x6 -> x2, local copies, waits for them, and re-layouts: 8.54 us -> 0.06 us  [assemble(): pieces[:, 1, 1, :, :, FRONT + quarter - 16:, :].transpose(3, 0, 2, 1, 4)]
    add x13 -> x12, other arithmetic: 12.3 us -> 4.3 us  [add(): kept + got.astype(F32) * jnp.exp2(theirs).reshape((1,) * (got.ndim - 1) +...]
    ppermute x19 -> x18, starting transfers between devices: 14 us -> 22 us  [flip(): return lax.ppermute(array, axis, [(i, i ^ 1 << bit) for i in range(size)])]
    convert_element_type x10 -> x14, other arithmetic: 11.1 us -> 4.47 us  [the longest x13 4.41 us: encode(): return jnp.where(row == at, here, values * jnp.exp2(-here)).astype(F16)]
  transfers between devices with their start and end apart: 35 -> 26, of which waited for: 16 -> 17; matrix products, arithmetic and copies ran while one was open for 16% -> 7% of each run, Pallas kernels for 17% -> 25%
where the time goes in v2:
time: 264 us; the launch traced here: 261 us
  Pallas kernels  104 us (39%)
  waiting for transfers between devices  68.3 us (26%)
  starting transfers between devices  31.5 us (12%)
  other arithmetic  30.2 us (11%)
  local copies, waits for them, and re-layouts  24.2 us (9%)
    ppermute x18, waiting for transfers between devices, flip(): return lax.ppermute(array, axis, [(i, i ^ 1 << bit) for i in range(size)])  39.5 us
    pallas_call x1, Pallas kernels, layers(): pl.pallas_call(lambda *refs: layers_kernel((fields, emb, dense, len(chunk...  28.9 us
    ppermute x8, waiting for transfers between devices, crossed_flip(): lax.ppermute(array, ('dp', 'mp'), crossed_pairs(stage, lax.axis_size('dp'...  28.8 us
    pallas_call x2, Pallas kernels, weight_grads(): pl.pallas_call(lambda *refs: weight_kernel(rows, examples_all, *refs), gr...  25.1 us
    pallas_call x3, Pallas kernels, lookup(): pl.pallas_call(lambda *refs: lookup_kernel(emb, blocks, at_row, *refs), o...  23.7 us
    ppermute x18, starting transfers between devices, flip(): return lax.ppermute(array, axis, [(i, i ^ 1 << bit) for i in range(size)])  22 us
    pallas_call x2, Pallas kernels, spread(): pl.pallas_call(lambda *refs: spread_kernel(first, *refs), grid=(count //...  19.1 us
    unnamed x68, local copies, waits for them, and re-layouts  18.7 us
  transfers between devices with their start and end apart: 26, of which 17 were waited for; matrix products, arithmetic and copies ran while one was open for 7% of the time, Pallas kernels for 25%

profile of v2, /device:TPU:0, one launch (start us, length us, event | category | flops | bytes accessed | tf_op | source)
XLA Modules:
  0.0 260.5 jit_solution(9415138317305145142)
XLA Ops:
  0.7 2.8 %fusion.93 = (bf16[429,1024]{1,0:T(8,128)(2,1)}, bf16[429,1024]{1,0:T(8,128)(2,1)S(1)}) fusion(bf16[1014,1024]{1,0:T(8,128)(2,1)} %bitcast.372), kind=kLoop, calls=%fused_computation.224 | loop fusion | bytes 3514368 | tf_op jit(solution)/shard_map/slice | solution.py:699
  3.5 3.0 %collective-permute-start.1 = (bf16[429,1024]{1,0:T(8,128)(2,1)S(1)}, bf16[429,1024]{1,0:T(8,128)(2,1)}, u32[]{:S(2)}, u32[]{:S(2)}) collective-permute-start(bf16[429,1024]{1,0:T(8,128)(2,1)S(1)} %get-tuple-element.129), channel_id=1, source_target_pairs={{0,2},{1,3},{2,0},{3,1},{4,6},{5,7},{6,4},{7,5},{8,10},{9,11},{10,... | collective-permute-start | bytes 2635784 | tf_op jit(solution)/shard_map/ppermute | solution.py:513
  6.6 1.6 copy-done.5
  8.2 2.6 %prepare.1 = (bf16[2056,1032]{1,0:T(8,128)(2,1)S(1)}, bf16[1032,2056]{1,0:T(8,128)(2,1)S(1)}, f32[1032,128]{1,0:T(8,128)S(1)}, f32[1024,128]{1,0:T(8,128)S(1)}, ...) custom-call(bf16[1027,1027]{1,0:T(8,128)(2,1)S(1)} %copy-done.3, bf16[1027,1024]{1,0:T(8,128)(2,1)S(1)} %copy-done.5, ...), custom_call_target="tpu_custom_call" | custom-call | bytes 17040384 | tf_op jit(solution)/shard_map/prepare/pallas_call | solution.py:79
  10.8 2.2 copy-done.9
  13.0 2.1 copy-done.10
  18.3 8.7 %collective-permute-done.1.refs_4_ = bf16[429,1024]{1,0:T(8,128)(2,1)} collective-permute-done((bf16[429,1024]{1,0:T(8,128)(2,1)S(1)}, bf16[429,1024]{1,0:T(8,128)(2,1)}, u32[]{:S(2)}, u32[]{:S(2)}) %collective-permute-start.1) | collective-permute-done | bytes 878624 | tf_op jit(solution)/shard_map/ppermute | solution.py:513
  29.9 9.4 %lookup.3.refs_0_ = bf16[11,40,1536]{2,1,0:T(8,128)(2,1)S(1)} custom-call(s32[11,1536]{1,0:T(8,128)S(1)} %get-tuple-element.153.refs_0_, s32[11,1536]{1,0:T(8,128)S(1)} %get-tuple-element.142.refs_1_, bf16[1014,1024]{1,0:T(8,128)(2,1)S(1)} %bitcast.374, bf16[1014,1024]{1,0:T(8,128)(2,1)} %collective-permute-done.refs_3_, ...), custom_call_target="tpu_custom_call" | custom-call | flops 5536481280 | bytes 2703360 | tf_op jit(solution)/shard_map/lookup/pallas_call | solution.py:130
  39.3 5.8 %collective-permute-done.3.refs_4_ = bf16[429,1024]{1,0:T(8,128)(2,1)S(1)} collective-permute-done((bf16[429,1024]{1,0:T(8,128)(2,1)}, bf16[429,1024]{1,0:T(8,128)(2,1)S(1)}, u32[]{:S(2)}, u32[]{:S(2)}) %collective-permute-start.3) | collective-permute-done | bytes 878624 | tf_op jit(solution)/shard_map/ppermute | solution.py:513
  45.2 1.8 collective-permute-start.5
  47.5 9.2 %lookup.4.refs_1_ = bf16[11,40,1536]{2,1,0:T(8,128)(2,1)S(1)} custom-call(s32[11,1536]{1,0:T(8,128)S(1)} %get-tuple-element.154.refs_0_, s32[11,1536]{1,0:T(8,128)S(1)} %get-tuple-element.141.refs_1_, bf16[1014,1024]{1,0:T(8,128)(2,1)S(1)} %bitcast.376, bf16[1014,1024]{1,0:T(8,128)(2,1)} %collective-permute-done.refs_3_, ...), custom_call_target="tpu_custom_call" | custom-call | flops 5536481280 | bytes 2703360 | tf_op jit(solution)/shard_map/lookup/pallas_call | solution.py:130
  59.5 5.0 %lookup.5.refs_2_ = bf16[4,40,1536]{2,1,0:T(8,128)(2,1)S(1)} custom-call(s32[4,1536]{1,0:T(4,128)S(1)} %slice.160.refs_0_, s32[4,1536]{1,0:T(4,128)S(1)} %slice.161.refs_1_, bf16[1014,1024]{1,0:T(8,128)(2,1)S(1)} %bitcast.377, bf16[1014,1024]{1,0:T(8,128)(2,1)} %collective-permute-done.refs_3_, bf16[156,1024]{1,0:T(8,128)(2,1)S(1)} %collective-permute-done.5.refs_4_, ...), custom_call_target="tpu_custom_call" | custom-call | flops 2013265920 | bytes 983040 | tf_op jit(solution)/shard_map/lookup/pallas_call | solution.py:130
  64.6 28.9 %layers.1 = (f32[1,1536]{1,0:T(1,128)S(1)}, bf16[1040,1536]{1,0:T(8,128)(2,1)S(1)}, bf16[2064,1536]{1,0:T(8,128)(2,1)}, bf16[26,40,1536]{2,1,0:T(8,128)(2,1)}, f...) custom-call(bf16[11,40,1536]{2,1,0:T(8,128)(2,1)S(1)} %copy-done.22,, ...), custom_call_target="tpu_custom_call" | custom-call | flops 13036290048 | bytes 41140224 | tf_op jit(solution)/shard_map/layers/pallas_call | solution.py:326
  95.1 7.1 %weight_grads.2 = f32[4,4,528,128]{3,2,1,0:T(8,128)S(1)} custom-call(s32[1]{0:T(128)} %bitcast.5.refs_0_, bf16[1040,1536]{1,0:T(8,128)(2,1)S(1)} %get-tuple-element.68.refs_1_, bf16[2064,1536]{1,0:T(8,128)(2,1)} %get-tuple-element.69.refs_2_.refs_3_.refs_4_, bf16[2064,1536]{1,0:T(8,128)(2,1)} %get-tuple-element.69.refs_2_.refs_3_.refs_4_, ...), custom_call_target="tpu_custom_call" | custom-call | flops 3246391296 | bytes 10567680 | tf_op jit(solution)/shard_map/weight_grads/pallas_call | solution.py:424
  102.2 2.0 select_convert_fusion
  104.6 2.7 %fusion.26 = (s32[26,3072]{1,0:T(8,128)S(1)}, s32[26,3072]{1,0:T(8,128)S(1)}) fusion(s32[26,6144]{1,0:T(8,128)} %compare_select_fusion, s32[]{:T(128)S(6)} %select_n.261, s32[]{:T(128)} %and.103, pred[]{:T(512)S(6)} %eq.112), kind=kLoop, calls=%fused_computation.85 | loop fusion | flops 8706048 | bytes 958473 | tf_op jit(solution)/shard_map/jit(_where)/select_n | solution.py:659
  107.4 18.0 %weight_grads.3 = f32[4,4,528,128]{3,2,1,0:T(8,128)S(1)} custom-call(s32[1]{0:T(128)} %bitcast.6.refs_0_, bf16[1040,1536]{1,0:T(8,128)(2,1)S(1)} %get-tuple-element.68.refs_1_, bf16[2064,1536]{1,0:T(8,128)(2,1)} %get-tuple-element.69.refs_2_.refs_3_.refs_4_, bf16[2064,1536]{1,0:T(8,128)(2,1)} %get-tuple-element.69.refs_2_.refs_3_.refs_4_, ...), custom_call_target="tpu_custom_call" | custom-call | flops 3246391296 | bytes 10567680 | tf_op jit(solution)/shard_map/weight_grads/pallas_call | solution.py:424
  126.1 2.2 multiply_add_fusion
  128.6 1.8 collective-permute-start.8
  130.4 8.9 %spread.2 = (f32[2,4,2,480,128]{4,3,2,1,0:T(8,128)S(1)}, f32[8,128]{1,0:T(8,128)S(1)}) custom-call(s32[1]{0:T(128)} %bitcast.14.refs_0_, s32[26,3072]{1,0:T(8,128)S(1)} %get-tuple-element.133.refs_1_, s32[26,3072]{1,0:T(8,128)S(1)} %get-tuple-element.132.refs_2_, bf16[26,40,1536]{2,1,0:T(8,128)(2,1)} %get-tuple-element.80.refs_3_, ...), custom_call_target="tpu_custom_call" | custom-call | flops 6039797760 | bytes 15728640 | tf_op jit(solution)/shard_map/spread/pallas_call | solution.py:491
  140.1 3.8 %collective-permute-done.8 = f16[2,4,528,128]{3,2,1,0:T(8,128)(2,1)S(1)} collective-permute-done((f16[2,4,528,128]{3,2,1,0:T(8,128)(2,1)S(1)}, f16[2,4,528,128]{3,2,1,0:T(8,128)(2,1)S(1)}, u32[]{:S(2)}, u32[]{:S(2)}) %collective-permute-start.8) | collective-permute-done | bytes 1081376 | tf_op jit(solution)/shard_map/ppermute | solution.py:531
  145.1 1.8 collective-permute-start.10
  146.9 10.2 %spread.3 = (f32[2,4,2,560,128]{4,3,2,1,0:T(8,128)S(1)}, f32[8,128]{1,0:T(8,128)S(1)}) custom-call(s32[1]{0:T(128)} %bitcast.14.refs_0_, s32[26,3072]{1,0:T(8,128)S(1)} %get-tuple-element.133.refs_1_, s32[26,3072]{1,0:T(8,128)S(1)} %get-tuple-element.132.refs_2_, bf16[26,40,1536]{2,1,0:T(8,128)(2,1)} %get-tuple-element.80.refs_3_, ...), custom_call_target="tpu_custom_call" | custom-call | flops 7046430720 | bytes 18350080 | tf_op jit(solution)/shard_map/spread/pallas_call | solution.py:491
  157.5 1.6 collective-permute-start.15
  160.4 2.1 collective-permute-start.11
  162.9 1.6 collective-permute-start.14
  164.5 3.7 %collective-permute-done.11 = f16[2,528,128]{2,1,0:T(8,128)(2,1)S(1)} collective-permute-done((f16[2,528,128]{2,1,0:T(8,128)(2,1)S(1)}, f16[2,528,128]{2,1,0:T(8,128)(2,1)S(1)}, u32[]{:S(2)}, u32[]{:S(2)}) %collective-permute-start.11) | collective-permute-done | bytes 270368 | tf_op jit(solution)/shard_map/ppermute | solution.py:513
  169.1 2.8 %collective-permute-start.13 = (f16[528,128]{1,0:T(8,128)(2,1)S(1)}, f16[528,128]{1,0:T(8,128)(2,1)S(1)}, u32[]{:S(2)}, u32[]{:S(2)}) collective-permute-start(f16[528,128]{1,0:T(8,128)(2,1)S(1)} %fusion.36), channel_id=1, source_target_pairs={{0,16},{4,20},{8,24},{12,28},{16,0},{20,4},{24,8},{28,12},{1,17},{... | collective-permute-start | bytes 405512 | tf_op jit(solution)/shard_map/ppermute | solution.py:513
  171.9 6.8 %collective-permute-done.15 = f16[2,2,2,560,128]{4,3,2,1,0:T(8,128)(2,1)S(1)} collective-permute-done((f16[2,2,2,560,128]{4,3,2,1,0:T(8,128)(2,1)S(1)}, f16[2,2,2,560,128]{4,3,2,1,0:T(8,128)(2,1)S(1)}, u32[]{:S(2)}, u32[]{:S(2)}) %collective-permute-start.15) | collective-permute-done | bytes 1146912 | tf_op jit(solution)/shard_map/ppermute | solution.py:531
  180.3 1.6 collective-permute-start.17
  182.1 2.7 %collective-permute-start.16 = (f16[528,128]{1,0:T(8,128)(2,1)S(1)}, f16[528,128]{1,0:T(8,128)(2,1)S(1)}, u32[]{:S(2)}, u32[]{:S(2)}) collective-permute-start(f16[528,128]{1,0:T(8,128)(2,1)S(1)} %fusion.38), channel_id=1, source_target_pairs={{0,16},{4,20},{8,24},{12,28},{16,0},{20,4},{24,8},{28,12},{1,17},{... | collective-permute-start | bytes 405512 | tf_op jit(solution)/shard_map/ppermute | solution.py:513
  184.7 4.2 %collective-permute-done.18 = f16[2,2,560,128]{3,2,1,0:T(8,128)(2,1)S(1)} collective-permute-done((f16[2,2,560,128]{3,2,1,0:T(8,128)(2,1)S(1)}, f16[2,2,560,128]{3,2,1,0:T(8,128)(2,1)S(1)}, u32[]{:S(2)}, u32[]{:S(2)}) %collective-permute-start.18) | collective-permute-done | bytes 573472 | tf_op jit(solution)/shard_map/ppermute | solution.py:531
  191.2 3.4 %collective-permute-start.22 = (f16[480,128]{1,0:T(8,128)(2,1)S(1)}, f16[480,128]{1,0:T(8,128)(2,1)S(1)}, u32[]{:S(2)}, u32[]{:S(2)}) collective-permute-start(f16[480,128]{1,0:T(8,128)(2,1)S(1)} %fusion.41), channel_id=1, source_target_pairs={{0,16},{4,20},{8,24},{12,28},{16,0},{20,4},{24,8},{28,12},{1,17},{... | collective-permute-start | bytes 368648 | tf_op jit(solution)/shard_map/ppermute | solution.py:513
  194.8 7.3 %collective-permute-done.20 = f16[2,560,128]{2,1,0:T(8,128)(2,1)S(1)} collective-permute-done((f16[2,560,128]{2,1,0:T(8,128)(2,1)S(1)}, f16[2,560,128]{2,1,0:T(8,128)(2,1)S(1)}, u32[]{:S(2)}, u32[]{:S(2)}) %collective-permute-start.20) | collective-permute-done | bytes 286752 | tf_op jit(solution)/shard_map/ppermute | solution.py:513
  202.3 3.0 %collective-permute-done.19 = f16[2,528,128]{2,1,0:T(8,128)(2,1)S(1)} collective-permute-done((f16[2,528,128]{2,1,0:T(8,128)(2,1)S(1)}, f16[2,528,128]{2,1,0:T(8,128)(2,1)S(1)}, u32[]{:S(2)}, u32[]{:S(2)}) %collective-permute-start.19) | collective-permute-done | bytes 270368 | tf_op jit(solution)/shard_map/ppermute | solution.py:513
  205.7 1.5 collective-permute-start.21
  208.0 7.3 %collective-permute-done.21 = f16[2,2,528,128]{3,2,1,0:T(8,128)(2,1)} collective-permute-done((f16[2,2,528,128]{3,2,1,0:T(8,128)(2,1)S(1)}, f16[2,2,528,128]{3,2,1,0:T(8,128)(2,1)}, u32[]{:S(2)}, u32[]{:S(2)}) %collective-permute-start.21) | collective-permute-done | bytes 540704 | tf_op jit(solution)/shard_map/ppermute | solution.py:531
  215.2 1.4 select_bitcast_fusion.5
  218.0 3.1 %collective-permute-start.24 = (f16[560,128]{1,0:T(8,128)(2,1)S(1)}, f16[560,128]{1,0:T(8,128)(2,1)S(1)}, u32[]{:S(2)}, u32[]{:S(2)}) collective-permute-start(f16[560,128]{1,0:T(8,128)(2,1)S(1)} %fusion.34), channel_id=1, source_target_pairs={{0,16},{4,20},{8,24},{12,28},{16,0},{20,4},{24,8},{28,12},{1,17},{... | collective-permute-start | bytes 430088 | tf_op jit(solution)/shard_map/ppermute | solution.py:513
  221.1 5.7 %collective-permute-done.24 = f16[560,128]{1,0:T(8,128)(2,1)S(1)} collective-permute-done((f16[560,128]{1,0:T(8,128)(2,1)S(1)}, f16[560,128]{1,0:T(8,128)(2,1)S(1)}, u32[]{:S(2)}, u32[]{:S(2)}) %collective-permute-start.24) | collective-permute-done | bytes 143392 | tf_op jit(solution)/shard_map/ppermute | solution.py:513
  226.9 6.4 %collective-permute-done.23 = f16[2,2,2,528,128]{4,3,2,1,0:T(8,128)(2,1)} collective-permute-done((f16[2,2,2,528,128]{4,3,2,1,0:T(8,128)(2,1)}, f16[2,2,2,528,128]{4,3,2,1,0:T(8,128)(2,1)}, u32[]{:S(2)}, u32[]{:S(2)}) %collective-permute-start.23) | collective-permute-done | bytes 1081376 | tf_op jit(solution)/shard_map/ppermute | solution.py:531
  233.3 1.9 select_bitcast_fusion.3
  235.3 1.9 pad_maximum_fusion
  239.4 2.4 collective-permute-done.25
  241.8 3.1 %select_bitcast_fusion.1 = (f16[1,2,2,2,2,528,128]{6,5,4,3,2,1,0:T(8,128)(2,1)S(1)}, f16[1,2,2,2,2,528,128]{6,5,4,3,2,1,0:T(8,128)(2,1)S(1)}) fusion(f16[2,2,2,2,528,128]{5,4,3,2,1,0:T(8,128)(2,1)} %collective-permute-done.25, pred[]{:T(512)S(6)} %eq.112, f16[1,2,2,2,528,128]{5,4,3,2,1,0:T(8,128)(2,1)S(1)} %get-tuple-element.126, ...), kind=kLoop, calls=%fused_computation.13 | loop fusion | flops 3244032 | bytes 8650753 | tf_op jit(solution)/shard_map/stack | solution.py:573
  246.0 3.4 %copy-done = f32[2,2,2,2,2,528,128]{6,5,4,3,2,1,0:T(8,128)} copy-done((f32[2,2,2,2,2,528,128]{6,5,4,3,2,1,0:T(8,128)}, f32[2,2,2,2,2,528,128]{6,5,4,3,2,1,0:T(8,128)S(1)}, u32[]{:S(2)}) %copy-start) | copy-done | bytes 8650776
  249.9 3.4 %copy-done.1 = f32[2,2,2,2,2,528,128]{6,5,4,3,2,1,0:T(8,128)S(1)} copy-done((f32[2,2,2,2,2,528,128]{6,5,4,3,2,1,0:T(8,128)S(1)}, f32[2,2,2,2,2,528,128]{6,5,4,3,2,1,0:T(8,128)}, u32[]{:S(2)}) %copy-start.1) | copy-done | bytes 8650776
  253.3 4.6 %assemble.1 = (f32[1027,1027]{1,0:T(8,128)}, f32[1027,1024]{1,0:T(8,128)}, f32[8,1024]{1,0:T(8,128)S(1)}) custom-call(f32[2,2,2,2,2,528,128]{6,5,4,3,2,1,0:T(8,128)S(1)} %copy-done.1, f32[1032,128]{1,0:T(8,128)S(1)} %pad.13.refs_1_), custom_call_target="tpu_custom_call" | custom-call | bytes 16908288 | tf_op jit(solution)/shard_map/assemble/pallas_call | solution.py:620
  (182 shorter events, 29.6 us)
Async XLA Ops:
  0.6 5.9 %copy-start.32 = (f32[1027]{0:T(1024)S(1)}, f32[1027]{0:T(1024)}, u32[]{:S(2)}) copy-start(f32[1027]{0:T(1024)} %param.20) | copy-start | bytes 12328
  0.7 5.9 %copy-start.33 = (f32[1027]{0:T(1024)S(1)}, f32[1027]{0:T(1024)}, u32[]{:S(2)}) copy-start(f32[1027]{0:T(1024)} %param.23) | copy-start | bytes 12328
  0.7 5.9 %copy-start.7 = (f32[1024]{0:T(1024)S(1)}, f32[1024]{0:T(1024)}, u32[]{:S(2)}) copy-start(f32[1024]{0:T(1024)} %param.22) | copy-start | bytes 12292
  0.7 5.9 %copy-start.8 = (f32[1024]{0:T(1024)S(1)}, f32[1024]{0:T(1024)}, u32[]{:S(2)}) copy-start(f32[1024]{0:T(1024)} %param.24) | copy-start | bytes 12292
  0.7 5.9 %copy-start.3 = (bf16[1027,1027]{1,0:T(8,128)(2,1)S(1)}, bf16[1027,1027]{1,0:T(8,128)(2,1)}, u32[]{:S(2)}) copy-start(bf16[1027,1027]{1,0:T(8,128)(2,1)} %cw_ref.1) | copy-start | bytes 6328378
  3.5 23.5 %collective-permute-start.1 = (bf16[429,1024]{1,0:T(8,128)(2,1)S(1)}, bf16[429,1024]{1,0:T(8,128)(2,1)}, u32[]{:S(2)}, u32[]{:S(2)}) collective-permute-start(bf16[429,1024]{1,0:T(8,128)(2,1)S(1)} %get-tuple-element.129), channel_id=1, source_target_pairs={{0,2},{1,3},{2,0},{3,1},{4,6},{5,7},{6,4},{7,5},{8,10},{9,11},{10,... | collective-permute-start | bytes 2635784 | tf_op jit(solution)/shard_map/ppermute | solution.py:513
  6.5 23.4 %collective-permute-start = (bf16[1014,1024]{1,0:T(8,128)(2,1)}, bf16[1014,1024]{1,0:T(8,128)(2,1)}, u32[]{:S(2)}, u32[]{:S(2)}) collective-permute-start(bf16[1014,1024]{1,0:T(8,128)(2,1)} %bitcast.373), channel_id=1, source_target_pairs={{0,1},{1,0},{2,3},{3,2},{4,5},{5,4},{6,7},{7,6},{8,9},{9,8},{10,11... | collective-permute-start | bytes 6230024 | tf_op jit(solution)/shard_map/ppermute | solution.py:513
  6.5 38.6 %collective-permute-start.3 = (bf16[429,1024]{1,0:T(8,128)(2,1)}, bf16[429,1024]{1,0:T(8,128)(2,1)S(1)}, u32[]{:S(2)}, u32[]{:S(2)}) collective-permute-start(bf16[429,1024]{1,0:T(8,128)(2,1)} %get-tuple-element.128), channel_id=1, source_target_pairs={{0,2},{1,3},{2,0},{3,1},{4,6},{5,7},{6,4},{7,5},{8,10},{9,11},{10,... | collective-permute-start | bytes 2635784 | tf_op jit(solution)/shard_map/ppermute | solution.py:513
  8.2 18.9 %copy-start.26 = (s32[26,6144]{1,0:T(8,128)S(1)}, s32[26,6144]{1,0:T(8,128)}, u32[]{:S(2)}) copy-start(s32[26,6144]{1,0:T(8,128)} %param.13) | copy-start | bytes 1916932
  8.2 18.9 %copy-start.27 = (s32[26,6144]{1,0:T(8,128)S(1)}, s32[26,6144]{1,0:T(8,128)}, u32[]{:S(2)}) copy-start(s32[26,6144]{1,0:T(8,128)} %param.14) | copy-start | bytes 1916932
  18.3 11.5 %copy-start.4 = (bf16[1024,1014]{0,1:T(8,128)(2,1)S(1)}, bf16[1024,1014]{0,1:T(8,128)(2,1)}, u32[]{:S(2)}) copy-start(bf16[1024,1014]{0,1:T(8,128)(2,1)} %param.18) | copy-start | bytes 6230020
  27.1 2.8 %collective-permute-start.2 = (bf16[429,1024]{1,0:T(8,128)(2,1)}, bf16[429,1024]{1,0:T(8,128)(2,1)}, u32[]{:S(2)}, u32[]{:S(2)}) collective-permute-start(bf16[429,1024]{1,0:T(8,128)(2,1)} %collective-permute-done.1.refs_4_), channel_id=1, source_target_pairs={{0,1},{1,0},{2,3},{3,2},{4,5},{5,4},{6,7},{7,6},{8,9},{9,8},{10,11... | collective-permute-start | bytes 2635784 | tf_op jit(solution)/shard_map/ppermute | solution.py:513
  39.3 17.4 %copy-start.21 = (bf16[11,40,1536]{2,1,0:T(8,128)(2,1)}, bf16[11,40,1536]{2,1,0:T(8,128)(2,1)S(1)}, u32[]{:S(2)}) copy-start(bf16[11,40,1536]{2,1,0:T(8,128)(2,1)S(1)} %lookup.3.refs_0_) | copy-start | bytes 4055044
  45.1 2.4 collective-permute-start.4
  45.2 12.6 %collective-permute-start.5 = (bf16[156,1024]{1,0:T(8,128)(2,1)S(1)}, bf16[156,1024]{1,0:T(8,128)(2,1)S(1)}, u32[]{:S(2)}, u32[]{:S(2)}) collective-permute-start(bf16[156,1024]{1,0:T(8,128)(2,1)S(1)} %slice.162), channel_id=1, source_target_pairs={{0,2},{1,3},{2,0},{3,1},{4,6},{5,7},{6,4},{7,5},{8,10},{9,11},{10,... | collective-permute-start | bytes 958472 | tf_op jit(solution)/shard_map/ppermute | solution.py:513
  47.5 10.5 %copy-start.31 = (s32[1536]{0:T(1024)S(1)}, s32[1536]{0:T(1024)}, u32[]{:S(2)}) copy-start(s32[1536]{0:T(1024)} %param.17) | copy-start | bytes 18436
  57.8 1.6 collective-permute-start.6
  58.7 5.8 %copy-start.12 = (f32[1032,128]{1,0:T(8,128)S(1)}, f32[1032,128]{1,0:T(8,128)}, u32[]{:S(2)}) copy-start(f32[1032,128]{1,0:T(8,128)} %copy-done.11) | copy-start | bytes 1585156
  58.7 5.8 %copy-start.14 = (f32[1032,128]{1,0:T(8,128)S(1)}, f32[1032,128]{1,0:T(8,128)}, u32[]{:S(2)}) copy-start(f32[1032,128]{1,0:T(8,128)} %copy-done.13) | copy-start | bytes 1585156
  58.7 5.8 %copy-start.16 = (f32[1024,128]{1,0:T(8,128)S(1)}, f32[1024,128]{1,0:T(8,128)}, u32[]{:S(2)}) copy-start(f32[1024,128]{1,0:T(8,128)} %copy-done.15) | copy-start | bytes 1572868
  58.7 5.8 %copy-start.18 = (f32[1024,128]{1,0:T(8,128)S(1)}, f32[1024,128]{1,0:T(8,128)}, u32[]{:S(2)}) copy-start(f32[1024,128]{1,0:T(8,128)} %copy-done.17) | copy-start | bytes 1572868
  58.7 5.8 %copy-start.19 = (f32[13,1536]{1,0:T(8,128)S(1)}, f32[13,1536]{1,0:T(8,128)}, u32[]{:S(2)}) copy-start(f32[13,1536]{1,0:T(8,128)} %refs_3_.1) | copy-start | bytes 239620
  58.7 5.8 %copy-start.20 = (s32[13,1536]{1,0:T(8,128)S(1)}, s32[13,1536]{1,0:T(8,128)}, u32[]{:S(2)}) copy-start(s32[13,1536]{1,0:T(8,128)} %refs_4_.1) | copy-start | bytes 239620
  58.8 5.8 %copy-start.22 = (bf16[11,40,1536]{2,1,0:T(8,128)(2,1)S(1)}, bf16[11,40,1536]{2,1,0:T(8,128)(2,1)}, u32[]{:S(2)}) copy-start(bf16[11,40,1536]{2,1,0:T(8,128)(2,1)} %copy-done.21) | copy-start | bytes 4055044
  58.8 5.8 %copy-start.24 = (bf16[11,40,1536]{2,1,0:T(8,128)(2,1)S(1)}, bf16[11,40,1536]{2,1,0:T(8,128)(2,1)}, u32[]{:S(2)}) copy-start(bf16[11,40,1536]{2,1,0:T(8,128)(2,1)} %copy-done.23) | copy-start | bytes 4055044
  95.1 35.4 %collective-permute-start.9 = (bf16[26,40,1536]{2,1,0:T(8,128)(2,1)}, bf16[26,40,1536]{2,1,0:T(8,128)(2,1)}, u32[]{:S(2)}, u32[]{:S(2)}) collective-permute-start(bf16[26,40,1536]{2,1,0:T(8,128)(2,1)} %get-tuple-element.80.refs_3_), channel_id=1, source_target_pairs={{0,1},{1,0},{2,3},{3,2},{4,5},{5,4},{6,7},{7,6},{8,9},{9,8},{10,11... | collective-permute-start | bytes 9584648 | tf_op jit(solution)/shard_map/ppermute | solution.py:513
  104.2 21.2 %collective-permute-start.7 = (f16[4,4,528,128]{3,2,1,0:T(8,128)(2,1)}, f16[4,4,528,128]{3,2,1,0:T(8,128)(2,1)}, u32[]{:S(2)}, u32[]{:S(2)}) collective-permute-start(f16[4,4,528,128]{3,2,1,0:T(8,128)(2,1)} %select_convert_fusion), channel_id=1, source_target_pairs={{0,1},{1,0},{2,3},{3,2},{4,5},{5,4},{6,7},{7,6},{8,9},{9,8},{10,11... | collective-permute-start | bytes 6488072 | tf_op jit(solution)/shard_map/ppermute | solution.py:513
  128.6 15.2 %collective-permute-start.8 = (f16[2,4,528,128]{3,2,1,0:T(8,128)(2,1)S(1)}, f16[2,4,528,128]{3,2,1,0:T(8,128)(2,1)S(1)}, u32[]{:S(2)}, u32[]{:S(2)}) collective-permute-start(f16[2,4,528,128]{3,2,1,0:T(8,128)(2,1)S(1)} %fusion.3), channel_id=1, source_target_pairs={{0,4},{1,3},{2,6},{3,1},{4,0},{5,7},{6,2},{7,5},{8,12},{9,11},{10,... | collective-permute-start | bytes 3244040 | tf_op jit(solution)/shard_map/ppermute | solution.py:531
  139.7 22.8 %collective-permute-start.12 = (f16[2,2,2,480,128]{4,3,2,1,0:T(8,128)(2,1)S(1)}, f16[2,2,2,480,128]{4,3,2,1,0:T(8,128)(2,1)S(1)}, u32[]{:S(2)}, u32[]{:S(2)}) collective-permute-start(f16[2,2,2,480,128]{4,3,2,1,0:T(8,128)(2,1)S(1)} %fusion.5), channel_id=1, source_target_pairs={{0,4},{1,3},{2,6},{3,1},{4,0},{5,7},{6,2},{7,5},{8,12},{9,11},{10,... | collective-permute-start | bytes 2949128 | tf_op jit(solution)/shard_map/ppermute | solution.py:531
  145.1 14.3 %collective-permute-start.10 = (f16[4,528,128]{2,1,0:T(8,128)(2,1)S(1)}, f16[4,528,128]{2,1,0:T(8,128)(2,1)S(1)}, u32[]{:S(2)}, u32[]{:S(2)}) collective-permute-start(f16[4,528,128]{2,1,0:T(8,128)(2,1)S(1)} %fusion.9), channel_id=1, source_target_pairs={{0,2},{1,5},{2,0},{3,7},{4,6},{5,1},{6,4},{7,3},{8,10},{9,13},{10,... | collective-permute-start | bytes 1622024 | tf_op jit(solution)/shard_map/ppermute | solution.py:531
  157.5 21.2 %collective-permute-start.15 = (f16[2,2,2,560,128]{4,3,2,1,0:T(8,128)(2,1)S(1)}, f16[2,2,2,560,128]{4,3,2,1,0:T(8,128)(2,1)S(1)}, u32[]{:S(2)}, u32[]{:S(2)}) collective-permute-start(f16[2,2,2,560,128]{4,3,2,1,0:T(8,128)(2,1)S(1)} %fusion.1), channel_id=1, source_target_pairs={{0,4},{1,3},{2,6},{3,1},{4,0},{5,7},{6,2},{7,5},{8,12},{9,11},{10,... | collective-permute-start | bytes 3440648 | tf_op jit(solution)/shard_map/ppermute | solution.py:531
  159.4 8.8 %copy-start.28 = (f16[4,528,128]{2,1,0:T(8,128)(2,1)}, f16[4,528,128]{2,1,0:T(8,128)(2,1)S(1)}, u32[]{:S(2)}) copy-start(f16[4,528,128]{2,1,0:T(8,128)(2,1)S(1)} %collective-permute-done.10) | copy-start | bytes 1622020
  160.4 7.8 %collective-permute-start.11 = (f16[2,528,128]{2,1,0:T(8,128)(2,1)S(1)}, f16[2,528,128]{2,1,0:T(8,128)(2,1)S(1)}, u32[]{:S(2)}, u32[]{:S(2)}) collective-permute-start(f16[2,528,128]{2,1,0:T(8,128)(2,1)S(1)} %fusion.15), channel_id=1, source_target_pairs={{0,8},{4,12},{8,0},{12,4},{16,24},{20,28},{24,16},{28,20},{1,9},{5... | collective-permute-start | bytes 811016 | tf_op jit(solution)/shard_map/ppermute | solution.py:513
  162.9 17.1 %collective-permute-start.14 = (f16[2,2,480,128]{3,2,1,0:T(8,128)(2,1)S(1)}, f16[2,2,480,128]{3,2,1,0:T(8,128)(2,1)S(1)}, u32[]{:S(2)}, u32[]{:S(2)}) collective-permute-start(f16[2,2,480,128]{3,2,1,0:T(8,128)(2,1)S(1)} %fusion.11), channel_id=1, source_target_pairs={{0,2},{1,5},{2,0},{3,7},{4,6},{5,1},{6,4},{7,3},{8,10},{9,13},{10,... | collective-permute-start | bytes 1474568 | tf_op jit(solution)/shard_map/ppermute | solution.py:531
  168.2 10.5 %copy-start.29 = (f16[2,528,128]{2,1,0:T(8,128)(2,1)}, f16[2,528,128]{2,1,0:T(8,128)(2,1)S(1)}, u32[]{:S(2)}) copy-start(f16[2,528,128]{2,1,0:T(8,128)(2,1)S(1)} %collective-permute-done.11) | copy-start | bytes 811012
  169.1 12.8 %collective-permute-start.13 = (f16[528,128]{1,0:T(8,128)(2,1)S(1)}, f16[528,128]{1,0:T(8,128)(2,1)S(1)}, u32[]{:S(2)}, u32[]{:S(2)}) collective-permute-start(f16[528,128]{1,0:T(8,128)(2,1)S(1)} %fusion.36), channel_id=1, source_target_pairs={{0,16},{4,20},{8,24},{12,28},{16,0},{20,4},{24,8},{28,12},{1,17},{... | collective-permute-start | bytes 405512 | tf_op jit(solution)/shard_map/ppermute | solution.py:513
  179.2 9.8 %collective-permute-start.18 = (f16[2,2,560,128]{3,2,1,0:T(8,128)(2,1)S(1)}, f16[2,2,560,128]{3,2,1,0:T(8,128)(2,1)S(1)}, u32[]{:S(2)}, u32[]{:S(2)}) collective-permute-start(f16[2,2,560,128]{3,2,1,0:T(8,128)(2,1)S(1)} %fusion.7), channel_id=1, source_target_pairs={{0,2},{1,5},{2,0},{3,7},{4,6},{5,1},{6,4},{7,3},{8,10},{9,13},{10,... | collective-permute-start | bytes 1720328 | tf_op jit(solution)/shard_map/ppermute | solution.py:531
  180.3 9.9 %collective-permute-start.17 = (f16[2,480,128]{2,1,0:T(8,128)(2,1)S(1)}, f16[2,480,128]{2,1,0:T(8,128)(2,1)S(1)}, u32[]{:S(2)}, u32[]{:S(2)}) collective-permute-start(f16[2,480,128]{2,1,0:T(8,128)(2,1)S(1)} %fusion.17), channel_id=1, source_target_pairs={{0,8},{4,12},{8,0},{12,4},{16,24},{20,28},{24,16},{28,20},{1,9},{5... | collective-permute-start | bytes 737288 | tf_op jit(solution)/shard_map/ppermute | solution.py:513
  182.0 9.1 %copy-start.30 = (f16[528,128]{1,0:T(8,128)(2,1)}, f16[528,128]{1,0:T(8,128)(2,1)S(1)}, u32[]{:S(2)}) copy-start(f16[528,128]{1,0:T(8,128)(2,1)S(1)} %collective-permute-done.13) | copy-start | bytes 405508
  182.1 12.5 %collective-permute-start.16 = (f16[528,128]{1,0:T(8,128)(2,1)S(1)}, f16[528,128]{1,0:T(8,128)(2,1)S(1)}, u32[]{:S(2)}, u32[]{:S(2)}) collective-permute-start(f16[528,128]{1,0:T(8,128)(2,1)S(1)} %fusion.38), channel_id=1, source_target_pairs={{0,16},{4,20},{8,24},{12,28},{16,0},{20,4},{24,8},{28,12},{1,17},{... | collective-permute-start | bytes 405512 | tf_op jit(solution)/shard_map/ppermute | solution.py:513
  190.2 11.8 %collective-permute-start.20 = (f16[2,560,128]{2,1,0:T(8,128)(2,1)S(1)}, f16[2,560,128]{2,1,0:T(8,128)(2,1)S(1)}, u32[]{:S(2)}, u32[]{:S(2)}) collective-permute-start(f16[2,560,128]{2,1,0:T(8,128)(2,1)S(1)} %fusion.13), channel_id=1, source_target_pairs={{0,8},{4,12},{8,0},{12,4},{16,24},{20,28},{24,16},{28,20},{1,9},{5... | collective-permute-start | bytes 860168 | tf_op jit(solution)/shard_map/ppermute | solution.py:513
  191.2 16.0 %collective-permute-start.22 = (f16[480,128]{1,0:T(8,128)(2,1)S(1)}, f16[480,128]{1,0:T(8,128)(2,1)S(1)}, u32[]{:S(2)}, u32[]{:S(2)}) collective-permute-start(f16[480,128]{1,0:T(8,128)(2,1)S(1)} %fusion.41), channel_id=1, source_target_pairs={{0,16},{4,20},{8,24},{12,28},{16,0},{20,4},{24,8},{28,12},{1,17},{... | collective-permute-start | bytes 368648 | tf_op jit(solution)/shard_map/ppermute | solution.py:513
  194.7 10.6 %collective-permute-start.19 = (f16[2,528,128]{2,1,0:T(8,128)(2,1)S(1)}, f16[2,528,128]{2,1,0:T(8,128)(2,1)S(1)}, u32[]{:S(2)}, u32[]{:S(2)}) collective-permute-start(f16[2,528,128]{2,1,0:T(8,128)(2,1)S(1)} %pad_maximum_fusion.4), channel_id=1, source_target_pairs={{0,8},{4,12},{8,0},{12,4},{16,24},{20,28},{24,16},{28,20},{1,9},{5... | collective-permute-start | bytes 811016 | tf_op jit(solution)/shard_map/ppermute | solution.py:513
  205.7 9.5 %collective-permute-start.21 = (f16[2,2,528,128]{3,2,1,0:T(8,128)(2,1)S(1)}, f16[2,2,528,128]{3,2,1,0:T(8,128)(2,1)}, u32[]{:S(2)}, u32[]{:S(2)}) collective-permute-start(f16[2,2,528,128]{3,2,1,0:T(8,128)(2,1)S(1)} %pad_maximum_fusion.2), channel_id=1, source_target_pairs={{0,2},{1,5},{2,0},{3,7},{4,6},{5,1},{6,4},{7,3},{8,10},{9,13},{10,... | collective-permute-start | bytes 1622024 | tf_op jit(solution)/shard_map/ppermute | solution.py:531
  217.9 15.5 %collective-permute-start.23 = (f16[2,2,2,528,128]{4,3,2,1,0:T(8,128)(2,1)}, f16[2,2,2,528,128]{4,3,2,1,0:T(8,128)(2,1)}, u32[]{:S(2)}, u32[]{:S(2)}) collective-permute-start(f16[2,2,2,528,128]{4,3,2,1,0:T(8,128)(2,1)} %pad_maximum_fusion.1), channel_id=1, source_target_pairs={{0,4},{1,3},{2,6},{3,1},{4,0},{5,7},{6,2},{7,5},{8,12},{9,11},{10,... | collective-permute-start | bytes 3244040 | tf_op jit(solution)/shard_map/ppermute | solution.py:531
  218.0 8.8 %collective-permute-start.24 = (f16[560,128]{1,0:T(8,128)(2,1)S(1)}, f16[560,128]{1,0:T(8,128)(2,1)S(1)}, u32[]{:S(2)}, u32[]{:S(2)}) collective-permute-start(f16[560,128]{1,0:T(8,128)(2,1)S(1)} %fusion.34), channel_id=1, source_target_pairs={{0,16},{4,20},{8,24},{12,28},{16,0},{20,4},{24,8},{28,12},{1,17},{... | collective-permute-start | bytes 430088 | tf_op jit(solution)/shard_map/ppermute | solution.py:513
  237.2 4.6 %collective-permute-start.25 = (f16[2,2,2,2,528,128]{5,4,3,2,1,0:T(8,128)(2,1)}, f16[2,2,2,2,528,128]{5,4,3,2,1,0:T(8,128)(2,1)}, u32[]{:S(2)}, u32[]{:S(2)}) collective-permute-start(f16[2,2,2,2,528,128]{5,4,3,2,1,0:T(8,128)(2,1)} %pad_maximum_fusion), channel_id=1, source_target_pairs={{0,1},{1,0},{2,3},{3,2},{4,5},{5,4},{6,7},{7,6},{8,9},{9,8},{10,11... | collective-permute-start | bytes 6488072 | tf_op jit(solution)/shard_map/ppermute | solution.py:513
  249.8 3.5 %copy-start.1 = (f32[2,2,2,2,2,528,128]{6,5,4,3,2,1,0:T(8,128)S(1)}, f32[2,2,2,2,2,528,128]{6,5,4,3,2,1,0:T(8,128)}, u32[]{:S(2)}) copy-start(f32[2,2,2,2,2,528,128]{6,5,4,3,2,1,0:T(8,128)} %copy-done) | copy-start | bytes 25952260
  (12 other events, 18.5 us)
